TPU v7x, 512 devices: a whole 4x4x16 slice. The times are simulated.
512 devices in a mesh: ctx: 64 (over y, x, z_hi), head: 8 (over z_lo, core).
Axes of the slice: x: 4, y: 4, z: 16 (z_hi: 4, z_lo: 4; z = z_hi * 4 + z_lo), core: 2. Of those that a mesh axis runs over, the one named last changes fastest.
Arguments:
- inputs: bfloat16 [8192, 2304], P('ctx', 'head'), may hold values from -0.15625 to 0.15625
- queries: bfloat16 [8192, 2048], P('ctx', 'head'), may hold values from -18 to 18
- keys: bfloat16 [8192, 1024], P('ctx', 'head'), may hold values from -6 to 6
- values: bfloat16 [8192, 1024], P('ctx', 'head'), may hold values from -6 to 6
- grad_out: bfloat16 [8192, 2048], P('ctx', 'head'), may hold values from -6 to 6
- w_query: bfloat16 [2304, 2048], P(None, 'head'), may hold values from -0.125 to 0.125
- w_key: bfloat16 [2304, 1024], P(None, 'head'), may hold values from -0.1875 to 0.1875
- w_value: bfloat16 [2304, 1024], P(None, 'head'), may hold values from -0.1875 to 0.1875
- doc_lengths: int32 [17], replicated, may hold values from 1 to 3072, 8192 in all
Outputs:
- grad_input: bfloat16 [8192, 2304], P('ctx', 'head')
- grad_key_weight: float32 [2304, 1024], P('ctx', 'head')
- grad_value_weight: float32 [2304, 1024], P('ctx', 'head')
Inputs may be any that keep to these rules, and one draw needn't show every extreme that they name: `doc_lengths`: the 17 lengths sum to 8192, and the longest is exactly 3072.
All inputs are finite; a program needn't handle non-finite values.
Results may differ from a plain program's by a relative error of at most 0.017.
Values may be sent and summed in bfloat16 or wider, within the bound.
No kernel may reach another device: no remote copies, remote signals or barrier semaphores. Data moves between devices by JAX's collectives and lax.ppermute only.
A program may use at most 64 MiB of HBM per device.

v0:
```python
import jax
import jax.numpy as jnp
from jax import lax
from jax.sharding import PartitionSpec as P

QUERY_SCALE = 1.0 / 12.0
SOFT_CAP = 50.0


def shifted(value, axis, steps):
    count = lax.axis_size(axis)
    initial, last = (max(0, -steps), min(count, count - steps))
    return lax.ppermute(value, axis, [(source, source + steps) for source in range(initial, last)])


def doc_ids(positions, doc_ends):
    return jnp.sum((doc_ends[None, :] <= positions[:, None]).astype(jnp.int32), axis=1)


def capped(query_part, key_part):
    raw = (
        jnp.einsum("thd,kd->htk", query_part, key_part, preferred_element_type=jnp.float32)
        * QUERY_SCALE
    )
    return SOFT_CAP * jnp.tanh(raw / SOFT_CAP)


def blocked(array, block_rows):
    return array.reshape((array.shape[0] // block_rows, block_rows) + array.shape[1:])


def keep_state(carry_state):
    return carry_state


def window_rows_of(tok_rows, reach_back, block_rows):
    window_rows = (reach_back + 1) * tok_rows
    padded_rows = (window_rows + block_rows - 1) // block_rows * block_rows
    return (window_rows, padded_rows)


def pull_window(keys, values, first_pos, doc_ends, reach_back, block_rows, mover):
    tok_rows, head_width = keys.shape
    window_rows, padded_rows = window_rows_of(tok_rows, reach_back, block_rows)
    key_pair = jnp.stack([keys, values])
    key_store = jnp.zeros((2, padded_rows, head_width), jnp.bfloat16)
    key_store = lax.dynamic_update_slice_in_dim(key_store, key_pair, reach_back * tok_rows, 1)

    def pull_keys(turn_index, carry_state):
        moving, stored = carry_state
        moving = mover(moving)
        stored = lax.dynamic_update_slice_in_dim(
            stored, moving, (reach_back - turn_index) * tok_rows, 1
        )
        return (moving, stored)

    _, key_store = lax.fori_loop(1, reach_back + 1, pull_keys, (key_pair, key_store))
    slot_index = jnp.arange(padded_rows, dtype=jnp.int32)
    key_pos = first_pos - reach_back * tok_rows + slot_index
    key_valid = (slot_index < window_rows) & (key_pos >= 0)
    key_seg = jnp.where(key_valid, doc_ids(key_pos, doc_ends), -1)
    return (key_store[0], key_store[1], key_pos, key_seg)


def key_totals(query, query_pos, query_seg, key_rows, value_rows, key_pos, key_seg, block_rows):
    head_count = query.shape[1]
    tok_rows = query.shape[0]
    head_width = query.shape[2]

    def step(carry_state, block_item):
        key_block, value_block, pos_block, seg_block = block_item
        allowed = (query_seg[:, None] == seg_block[None, :]) & (
            pos_block[None, :] <= query_pos[:, None]
        )

        def work(state_now):
            scores = capped(query, key_block)
            weights = jnp.where(allowed[None], jnp.exp(scores), 0.0)
            summed = state_now[0] + jnp.sum(weights, axis=-1)
            mixed = state_now[1] + jnp.einsum(
                "htk,kd->htd",
                weights.astype(jnp.bfloat16),
                value_block,
                preferred_element_type=jnp.float32,
            )
            return (summed, mixed)

        return (lax.cond(jnp.any(allowed), work, keep_state, carry_state), None)

    start_state = (
        jnp.zeros((head_count, tok_rows), jnp.float32),
        jnp.zeros((head_count, tok_rows, head_width), jnp.float32),
    )
    result, _ = lax.scan(
        step,
        start_state,
        (
            blocked(key_rows, block_rows),
            blocked(value_rows, block_rows),
            blocked(key_pos, block_rows),
            blocked(key_seg, block_rows),
        ),
    )
    return result


def key_grads(
    query,
    grad_heads,
    totals,
    deltas,
    query_pos,
    query_seg,
    key_rows,
    value_rows,
    key_pos,
    key_seg,
    block_rows,
):

    def step(carry_state, block_item):
        key_block, value_block, pos_block, seg_block = block_item
        allowed = (query_seg[:, None] == seg_block[None, :]) & (
            pos_block[None, :] <= query_pos[:, None]
        )

        def work(state_now):
            scores = capped(query, key_block)
            weights = jnp.where(allowed[None], jnp.exp(scores), 0.0)
            probs = weights / totals[:, :, None]
            grad_prob = jnp.einsum(
                "thd,kd->htk", grad_heads, value_block, preferred_element_type=jnp.float32
            )
            slope = (
                QUERY_SCALE
                * probs
                * (grad_prob - deltas[:, :, None])
                * (1.0 - (scores / SOFT_CAP) ** 2)
            ).astype(jnp.bfloat16)
            return state_now + jnp.einsum(
                "htk,kd->thd", slope, key_block, preferred_element_type=jnp.float32
            )

        return (lax.cond(jnp.any(allowed), work, keep_state, carry_state), None)

    result, _ = lax.scan(
        step,
        jnp.zeros(query.shape, jnp.float32),
        (
            blocked(key_rows, block_rows),
            blocked(value_rows, block_rows),
            blocked(key_pos, block_rows),
            blocked(key_seg, block_rows),
        ),
    )
    return result


def query_grads(
    key_rows,
    value_rows,
    key_pos,
    key_seg,
    query_all,
    grad_all,
    totals_all,
    deltas_all,
    query_pos,
    query_seg,
    block_rows,
):

    def step(carry_state, block_item):
        query_block, grad_block, total_block, delta_block, pos_block, seg_block = block_item
        allowed = (seg_block[:, None] == key_seg[None, :]) & (
            key_pos[None, :] <= pos_block[:, None]
        )

        def work(state_now):
            scores = capped(query_block, key_rows)
            weights = jnp.where(allowed[None], jnp.exp(scores), 0.0)
            probs = jnp.where(allowed[None], weights / total_block.T[:, :, None], 0.0)
            grad_prob = jnp.einsum(
                "qhd,kd->hqk", grad_block, value_rows, preferred_element_type=jnp.float32
            )
            slope = (
                QUERY_SCALE
                * probs
                * (grad_prob - delta_block.T[:, :, None])
                * (1.0 - (scores / SOFT_CAP) ** 2)
            ).astype(jnp.bfloat16)
            grad_key = state_now[0] + jnp.einsum(
                "hqk,qhd->kd", slope, query_block, preferred_element_type=jnp.float32
            )
            grad_value = state_now[1] + jnp.einsum(
                "hqk,qhd->kd",
                probs.astype(jnp.bfloat16),
                grad_block,
                preferred_element_type=jnp.float32,
            )
            return (grad_key, grad_value)

        return (lax.cond(jnp.any(allowed), work, keep_state, carry_state), None)

    empty = jnp.zeros(key_rows.shape, jnp.float32)
    result, _ = lax.scan(
        step,
        (empty, empty),
        (
            blocked(query_all, block_rows),
            blocked(grad_all, block_rows),
            blocked(totals_all, block_rows),
            blocked(deltas_all, block_rows),
            blocked(query_pos, block_rows),
            blocked(query_seg, block_rows),
        ),
    )
    return result


def shards(inputs, queries, keys, values, grad_out, w_query, w_key, w_value, doc_lengths):
    tok_rows = queries.shape[0]
    head_width = keys.shape[1]
    head_count = queries.shape[1] // head_width
    shard_count = lax.axis_size("ctx")
    seq_len = tok_rows * shard_count
    block_rows = min(512, seq_len)
    reach_back = 3 * shard_count // 8
    window_rows, padded_rows = window_rows_of(tok_rows, reach_back, block_rows)
    first_pos = lax.axis_index("ctx") * tok_rows
    doc_ends = jnp.cumsum(doc_lengths)
    row_index = jnp.arange(tok_rows, dtype=jnp.int32)
    own_pos = first_pos + row_index
    own_seg = doc_ids(own_pos, doc_ends)
    query = queries.reshape(tok_rows, head_count, head_width)
    grad_heads = grad_out.reshape(tok_rows, head_count, head_width)
    key_all, value_all, key_pos, key_seg = pull_window(
        keys,
        values,
        first_pos,
        doc_ends,
        reach_back,
        block_rows,
        lambda moving: shifted(moving, "ctx", 1),
    )
    summed, mixed = key_totals(
        query, own_pos, own_seg, key_all, value_all, key_pos, key_seg, block_rows
    )
    outputs = mixed / summed[:, :, None]
    deltas = jnp.sum(grad_heads.transpose(1, 0, 2).astype(jnp.float32) * outputs, axis=-1)
    grad_query = key_grads(
        query,
        grad_heads,
        summed,
        deltas,
        own_pos,
        own_seg,
        key_all,
        value_all,
        key_pos,
        key_seg,
        block_rows,
    )
    totals_rows = summed.T
    deltas_rows = deltas.T
    query_pair = jnp.stack([queries, grad_out])
    stats_pair = jnp.stack([totals_rows, deltas_rows])
    query_store = jnp.zeros((2, padded_rows, head_count * head_width), jnp.bfloat16)
    query_store = lax.dynamic_update_slice_in_dim(query_store, query_pair, 0, 1)
    stats_store = jnp.zeros((2, padded_rows, head_count), jnp.float32)
    stats_store = lax.dynamic_update_slice_in_dim(stats_store, stats_pair, 0, 1)

    def pull_queries(turn_index, carry_state):
        moving_rows, moving_stats, stored_rows, stored_stats = carry_state
        moving_rows = shifted(moving_rows, "ctx", -1)
        moving_stats = shifted(moving_stats, "ctx", -1)
        stored_rows = lax.dynamic_update_slice_in_dim(
            stored_rows, moving_rows, turn_index * tok_rows, 1
        )
        stored_stats = lax.dynamic_update_slice_in_dim(
            stored_stats, moving_stats, turn_index * tok_rows, 1
        )
        return (moving_rows, moving_stats, stored_rows, stored_stats)

    _, _, query_store, stats_store = lax.fori_loop(
        1, reach_back + 1, pull_queries, (query_pair, stats_pair, query_store, stats_store)
    )
    query_all = query_store[0]
    grad_all = query_store[1]
    totals_all = stats_store[0]
    deltas_all = stats_store[1]
    slot_index = jnp.arange(padded_rows, dtype=jnp.int32)
    query_pos = first_pos + slot_index
    query_valid = (slot_index < window_rows) & (query_pos < seq_len)
    query_seg = jnp.where(query_valid, doc_ids(query_pos, doc_ends), -1)
    query_rows_all = query_all.reshape(query_all.shape[0], head_count, head_width)
    grad_rows_all = grad_all.reshape(grad_all.shape[0], head_count, head_width)
    grad_key, grad_value = query_grads(
        keys,
        values,
        own_pos,
        own_seg,
        query_rows_all,
        grad_rows_all,
        totals_all,
        deltas_all,
        query_pos,
        query_seg,
        block_rows,
    )
    grad_query = grad_query.reshape(tok_rows, head_count * head_width).astype(jnp.bfloat16)
    grad_key = grad_key.astype(jnp.bfloat16)
    grad_value = grad_value.astype(jnp.bfloat16)
    contract = (((1,), (1,)), ((), ()))
    term = lax.dot_general(w_query, grad_query, contract, preferred_element_type=jnp.float32)
    term = term + lax.dot_general(w_key, grad_key, contract, preferred_element_type=jnp.float32)
    term = term + lax.dot_general(w_value, grad_value, contract, preferred_element_type=jnp.float32)
    input_sum = lax.psum_scatter(
        term.astype(jnp.bfloat16), "head", scatter_dimension=0, tiled=True
    ).astype(jnp.float32)
    grad_input = input_sum.T.astype(jnp.bfloat16)
    features = lax.all_gather(inputs, "head", axis=1, tiled=True)
    grad_both = jnp.concatenate([grad_key, grad_value], axis=1)
    weight_sum = lax.psum_scatter(
        lax.dot_general(
            features, grad_both, (((0,), (0,)), ((), ())), preferred_element_type=jnp.float32
        ),
        "ctx",
        scatter_dimension=0,
        tiled=True,
    )
    return (grad_input, weight_sum[:, :head_width], weight_sum[:, head_width:])


def solution(mesh):
    placed = (
        P("ctx", "head"),
        P("ctx", "head"),
        P("ctx", "head"),
        P("ctx", "head"),
        P("ctx", "head"),
        P(None, "head"),
        P(None, "head"),
        P(None, "head"),
        P(),
    )
    return jax.shard_map(
        shards,
        mesh=mesh,
        in_specs=placed,
        out_specs=(P("ctx", "head"), P("ctx", "head"), P("ctx", "head")),
        check_vma=False,
    )
```

profile of v0, /device:TPU:32, one launch (start us, length us, event | category | flops | bytes accessed | tf_op | source)
XLA Modules:
  0.0 1744.0 jit_solution(16030115161803272385)
XLA Ops:
  10.4 277.5 %while.74 = (s32[]{:T(128)}, bf16[2,128,128]{2,1,0:T(8,128)(2,1)S(1)}, bf16[2,3584,128]{2,1,0:T(8,128)(2,1)S(1)}, s32[]{:T(128)}, s32[]{:T(128)}, /*index=5*/s32[]{:T(128)}, s32[]{:T(128)}, s32[]{:T(128)}) while((s32[]{:T(128)}, bf16[2,128,128]{2,1,0:T(8,128)(2,1)S(1)}, bf16[2,3584,128]{2,1,0:T(8,128)(2,1)S(1)}, s32[]{:T(128)}, s32[]{:T(128)}, ...), condition=%wide.region_1.2_spmd, body=%wide.region_0.0_spmd.sunk | while | flops 7 | bytes 524475 | solution.py:57
  10.4 9.1 collective-permute-start
  19.5 3.4 collective-permute-done
  22.9 8.5 collective-permute-start
  33.4 8.3 collective-permute-start
  44.2 8.4 collective-permute-start
  54.5 8.3 collective-permute-start
  64.7 12.1 collective-permute-start
  78.7 10.0 collective-permute-start
  88.7 4.3 collective-permute-done
  93.1 8.3 collective-permute-start
  104.4 8.4 collective-permute-start
  114.7 9.2 collective-permute-start
  125.8 8.3 collective-permute-start
  136.0 10.7 collective-permute-start
  148.7 9.6 collective-permute-start
  158.4 3.3 collective-permute-done
  161.7 8.7 collective-permute-start
  170.5 3.5 collective-permute-done
  173.9 8.4 collective-permute-start
  184.9 8.4 collective-permute-start
  195.2 8.3 collective-permute-start
  205.4 8.3 collective-permute-start
  213.7 3.8 collective-permute-done
  217.6 8.4 collective-permute-start
  228.8 8.4 collective-permute-start
  239.9 8.4 collective-permute-start
  251.0 9.6 collective-permute-start
  260.6 3.7 collective-permute-done
  264.3 8.4 collective-permute-start
  275.4 10.3 collective-permute-start
  289.6 13.6 while.76
  305.8 461.8 %while.75 = (s32[]{:T(128)}, bf16[2,128,256]{2,1,0:T(8,128)(2,1)S(1)}, f32[2,128,2]{1,2,0:T(2,128)S(1)}, bf16[2,3584,256]{2,1,0:T(8,128)(2,1)}, f32[2,3584,2]{1,...) while((s32[]{:T(128)}, bf16[2,128,256]{2,1,0:T(8,128)(2,1)S(1)}, ...), condition=%wide.region_18.19_spmd, body=%wide.region_17.18_spmd.sunk | while | flops 6 | bytes 1065187 | solution.py:285
  308.4 12.5 collective-permute-done.2
  324.3 11.7 collective-permute-done.2
  339.3 15.8 collective-permute-done.2
  358.4 8.8 collective-permute-done.2
  370.5 12.2 collective-permute-done.2
  386.0 13.9 collective-permute-done.2
  403.2 18.4 %collective-permute-done.2 = f32[2,128,2]{1,2,0:T(2,128)S(1)} collective-permute-done((f32[2,128,2]{1,2,0:T(2,128)S(1)}, f32[2,128,2]{1,2,0:T(2,128)S(1)}, u32[]{:S(2)}, u32[]{:S(2)}) %collective-permute-start.2) | collective-permute-done | bytes 2080 | tf_op jit(solution)/shard_map/while/body/eval_jaxpr/ppermute | solution.py:13
  424.8 30.2 %collective-permute-done.2 = f32[2,128,2]{1,2,0:T(2,128)S(1)} collective-permute-done((f32[2,128,2]{1,2,0:T(2,128)S(1)}, f32[2,128,2]{1,2,0:T(2,128)S(1)}, u32[]{:S(2)}, u32[]{:S(2)}) %collective-permute-start.2) | collective-permute-done | bytes 2080 | tf_op jit(solution)/shard_map/while/body/eval_jaxpr/ppermute | solution.py:13
  458.4 13.5 collective-permute-done.2
  475.2 21.0 %collective-permute-done.2 = f32[2,128,2]{1,2,0:T(2,128)S(1)} collective-permute-done((f32[2,128,2]{1,2,0:T(2,128)S(1)}, f32[2,128,2]{1,2,0:T(2,128)S(1)}, u32[]{:S(2)}, u32[]{:S(2)}) %collective-permute-start.2) | collective-permute-done | bytes 2080 | tf_op jit(solution)/shard_map/while/body/eval_jaxpr/ppermute | solution.py:13
  499.4 16.2 collective-permute-done.2
  518.9 14.7 collective-permute-done.2
  536.9 17.3 collective-permute-done.2
  557.5 8.7 collective-permute-done.2
  569.5 19.4 %collective-permute-done.2 = f32[2,128,2]{1,2,0:T(2,128)S(1)} collective-permute-done((f32[2,128,2]{1,2,0:T(2,128)S(1)}, f32[2,128,2]{1,2,0:T(2,128)S(1)}, u32[]{:S(2)}, u32[]{:S(2)}) %collective-permute-start.2) | collective-permute-done | bytes 2080 | tf_op jit(solution)/shard_map/while/body/eval_jaxpr/ppermute | solution.py:13
  592.2 34.4 %collective-permute-done.2 = f32[2,128,2]{1,2,0:T(2,128)S(1)} collective-permute-done((f32[2,128,2]{1,2,0:T(2,128)S(1)}, f32[2,128,2]{1,2,0:T(2,128)S(1)}, u32[]{:S(2)}, u32[]{:S(2)}) %collective-permute-start.2) | collective-permute-done | bytes 2080 | tf_op jit(solution)/shard_map/while/body/eval_jaxpr/ppermute | solution.py:13
  629.9 14.5 collective-permute-done.2
  647.7 12.9 collective-permute-done.2
  663.9 18.0 %collective-permute-done.2 = f32[2,128,2]{1,2,0:T(2,128)S(1)} collective-permute-done((f32[2,128,2]{1,2,0:T(2,128)S(1)}, f32[2,128,2]{1,2,0:T(2,128)S(1)}, u32[]{:S(2)}, u32[]{:S(2)}) %collective-permute-start.2) | collective-permute-done | bytes 2080 | tf_op jit(solution)/shard_map/while/body/eval_jaxpr/ppermute | solution.py:13
  685.2 14.5 collective-permute-done.2
  702.9 12.9 collective-permute-done.2
  719.2 18.0 %collective-permute-done.2 = f32[2,128,2]{1,2,0:T(2,128)S(1)} collective-permute-done((f32[2,128,2]{1,2,0:T(2,128)S(1)}, f32[2,128,2]{1,2,0:T(2,128)S(1)}, u32[]{:S(2)}, u32[]{:S(2)}) %collective-permute-start.2) | collective-permute-done | bytes 2080 | tf_op jit(solution)/shard_map/while/body/eval_jaxpr/ppermute | solution.py:13
  740.5 14.4 collective-permute-done.2
  758.2 8.7 collective-permute-done.2
  767.6 3.6 fusion.121
  771.2 4.6 reshape_reshape_squeeze.6
  783.5 15.2 while.78
  785.1 4.3 conditional.11
  798.8 13.3 all_gather.3
  814.3 12.7 while.77
  832.4 901.7 %all-reduce.6.cloned.1.call-done = f32[2304,256]{0,1:T(8,128)} async-done(((f32[2304,256]{0,1:T(8,128)}), f32[2304,256]{0,1:T(8,128)}) %all-reduce.6.cloned.1.call-update) | async-done | bytes 2359312
  (395 shorter events, 175.0 us)
Async XLA Ops:
  8.0 1726.1 %all-reduce.6.cloned.1.call-start = ((), (), s32[]{:S(2)}) async-start(), calls=%async_computation.2 | async-start | bytes 4718592
  10.4 12.5 collective-permute-start
  33.4 10.8 collective-permute-start
  64.7 14.0 collective-permute-start
  78.7 14.3 collective-permute-start
  93.1 11.3 collective-permute-start
  114.7 11.1 collective-permute-start
  136.0 12.7 collective-permute-start
  148.7 13.0 collective-permute-start
  161.7 12.2 collective-permute-start
  173.9 10.9 collective-permute-start
  205.4 12.2 collective-permute-start
  217.6 11.1 collective-permute-start
  228.8 11.1 collective-permute-start
  239.9 11.1 collective-permute-start
  251.0 13.3 collective-permute-start
  264.3 11.0 collective-permute-start
  275.4 12.6 collective-permute-start
  305.8 15.2 collective-permute-start.1
  307.1 13.9 collective-permute-start.2
  321.7 14.3 collective-permute-start.1
  323.0 13.0 collective-permute-start.2
  336.7 18.5 %collective-permute-start.1 = (bf16[2,128,256]{2,1,0:T(8,128)(2,1)S(1)}, bf16[2,128,256]{2,1,0:T(8,128)(2,1)S(1)}, u32[]{:S(2)}, u32[]{:S(2)}) collective-permute-start(bf16[2,128,256]{2,1,0:T(8,128)(2,1)S(1)} %get-tuple-element.1409), channel_id=1, source_target_pairs={{8,0},{16,8},{24,16},{32,24},{40,32},{48,40},{56,48},{64,56},{72,6... | collective-permute-start | bytes 393224 | tf_op jit(solution)/shard_map/while/body/eval_jaxpr/ppermute | solution.py:13
  338.0 17.2 collective-permute-start.2
  355.8 11.4 collective-permute-start.1
  367.9 14.8 collective-permute-start.1
  369.2 13.5 collective-permute-start.2
  383.4 16.5 collective-permute-start.1
  384.7 15.2 collective-permute-start.2
  400.6 21.0 %collective-permute-start.1 = (bf16[2,128,256]{2,1,0:T(8,128)(2,1)S(1)}, bf16[2,128,256]{2,1,0:T(8,128)(2,1)S(1)}, u32[]{:S(2)}, u32[]{:S(2)}) collective-permute-start(bf16[2,128,256]{2,1,0:T(8,128)(2,1)S(1)} %get-tuple-element.1409), channel_id=1, source_target_pairs={{8,0},{16,8},{24,16},{32,24},{40,32},{48,40},{56,48},{64,56},{72,6... | collective-permute-start | bytes 393224 | tf_op jit(solution)/shard_map/while/body/eval_jaxpr/ppermute | solution.py:13
  401.9 19.7 %collective-permute-start.2 = (f32[2,128,2]{1,2,0:T(2,128)S(1)}, f32[2,128,2]{1,2,0:T(2,128)S(1)}, u32[]{:S(2)}, u32[]{:S(2)}) collective-permute-start(f32[2,128,2]{1,2,0:T(2,128)S(1)} %get-tuple-element.1410), channel_id=1, source_target_pairs={{8,0},{16,8},{24,16},{32,24},{40,32},{48,40},{56,48},{64,56},{72,6... | collective-permute-start | bytes 6152 | tf_op jit(solution)/shard_map/while/body/eval_jaxpr/ppermute | solution.py:13
  422.2 32.8 %collective-permute-start.1 = (bf16[2,128,256]{2,1,0:T(8,128)(2,1)S(1)}, bf16[2,128,256]{2,1,0:T(8,128)(2,1)S(1)}, u32[]{:S(2)}, u32[]{:S(2)}) collective-permute-start(bf16[2,128,256]{2,1,0:T(8,128)(2,1)S(1)} %get-tuple-element.1409), channel_id=1, source_target_pairs={{8,0},{16,8},{24,16},{32,24},{40,32},{48,40},{56,48},{64,56},{72,6... | collective-permute-start | bytes 393224 | tf_op jit(solution)/shard_map/while/body/eval_jaxpr/ppermute | solution.py:13
  423.5 31.5 %collective-permute-start.2 = (f32[2,128,2]{1,2,0:T(2,128)S(1)}, f32[2,128,2]{1,2,0:T(2,128)S(1)}, u32[]{:S(2)}, u32[]{:S(2)}) collective-permute-start(f32[2,128,2]{1,2,0:T(2,128)S(1)} %get-tuple-element.1410), channel_id=1, source_target_pairs={{8,0},{16,8},{24,16},{32,24},{40,32},{48,40},{56,48},{64,56},{72,6... | collective-permute-start | bytes 6152 | tf_op jit(solution)/shard_map/while/body/eval_jaxpr/ppermute | solution.py:13
  455.8 16.1 collective-permute-start.1
  457.0 14.8 collective-permute-start.2
  472.6 23.6 %collective-permute-start.1 = (bf16[2,128,256]{2,1,0:T(8,128)(2,1)S(1)}, bf16[2,128,256]{2,1,0:T(8,128)(2,1)S(1)}, u32[]{:S(2)}, u32[]{:S(2)}) collective-permute-start(bf16[2,128,256]{2,1,0:T(8,128)(2,1)S(1)} %get-tuple-element.1409), channel_id=1, source_target_pairs={{8,0},{16,8},{24,16},{32,24},{40,32},{48,40},{56,48},{64,56},{72,6... | collective-permute-start | bytes 393224 | tf_op jit(solution)/shard_map/while/body/eval_jaxpr/ppermute | solution.py:13
  473.8 22.3 %collective-permute-start.2 = (f32[2,128,2]{1,2,0:T(2,128)S(1)}, f32[2,128,2]{1,2,0:T(2,128)S(1)}, u32[]{:S(2)}, u32[]{:S(2)}) collective-permute-start(f32[2,128,2]{1,2,0:T(2,128)S(1)} %get-tuple-element.1410), channel_id=1, source_target_pairs={{8,0},{16,8},{24,16},{32,24},{40,32},{48,40},{56,48},{64,56},{72,6... | collective-permute-start | bytes 6152 | tf_op jit(solution)/shard_map/while/body/eval_jaxpr/ppermute | solution.py:13
  496.8 18.8 %collective-permute-start.1 = (bf16[2,128,256]{2,1,0:T(8,128)(2,1)S(1)}, bf16[2,128,256]{2,1,0:T(8,128)(2,1)S(1)}, u32[]{:S(2)}, u32[]{:S(2)}) collective-permute-start(bf16[2,128,256]{2,1,0:T(8,128)(2,1)S(1)} %get-tuple-element.1409), channel_id=1, source_target_pairs={{8,0},{16,8},{24,16},{32,24},{40,32},{48,40},{56,48},{64,56},{72,6... | collective-permute-start | bytes 393224 | tf_op jit(solution)/shard_map/while/body/eval_jaxpr/ppermute | solution.py:13
  498.1 17.5 %collective-permute-start.2 = (f32[2,128,2]{1,2,0:T(2,128)S(1)}, f32[2,128,2]{1,2,0:T(2,128)S(1)}, u32[]{:S(2)}, u32[]{:S(2)}) collective-permute-start(f32[2,128,2]{1,2,0:T(2,128)S(1)} %get-tuple-element.1410), channel_id=1, source_target_pairs={{8,0},{16,8},{24,16},{32,24},{40,32},{48,40},{56,48},{64,56},{72,6... | collective-permute-start | bytes 6152 | tf_op jit(solution)/shard_map/while/body/eval_jaxpr/ppermute | solution.py:13
  516.3 17.3 collective-permute-start.1
  517.6 16.0 collective-permute-start.2
  534.3 19.9 %collective-permute-start.1 = (bf16[2,128,256]{2,1,0:T(8,128)(2,1)S(1)}, bf16[2,128,256]{2,1,0:T(8,128)(2,1)S(1)}, u32[]{:S(2)}, u32[]{:S(2)}) collective-permute-start(bf16[2,128,256]{2,1,0:T(8,128)(2,1)S(1)} %get-tuple-element.1409), channel_id=1, source_target_pairs={{8,0},{16,8},{24,16},{32,24},{40,32},{48,40},{56,48},{64,56},{72,6... | collective-permute-start | bytes 393224 | tf_op jit(solution)/shard_map/while/body/eval_jaxpr/ppermute | solution.py:13
  535.6 18.6 %collective-permute-start.2 = (f32[2,128,2]{1,2,0:T(2,128)S(1)}, f32[2,128,2]{1,2,0:T(2,128)S(1)}, u32[]{:S(2)}, u32[]{:S(2)}) collective-permute-start(f32[2,128,2]{1,2,0:T(2,128)S(1)} %get-tuple-element.1410), channel_id=1, source_target_pairs={{8,0},{16,8},{24,16},{32,24},{40,32},{48,40},{56,48},{64,56},{72,6... | collective-permute-start | bytes 6152 | tf_op jit(solution)/shard_map/while/body/eval_jaxpr/ppermute | solution.py:13
  554.9 11.3 collective-permute-start.1
  566.9 22.0 %collective-permute-start.1 = (bf16[2,128,256]{2,1,0:T(8,128)(2,1)S(1)}, bf16[2,128,256]{2,1,0:T(8,128)(2,1)S(1)}, u32[]{:S(2)}, u32[]{:S(2)}) collective-permute-start(bf16[2,128,256]{2,1,0:T(8,128)(2,1)S(1)} %get-tuple-element.1409), channel_id=1, source_target_pairs={{8,0},{16,8},{24,16},{32,24},{40,32},{48,40},{56,48},{64,56},{72,6... | collective-permute-start | bytes 393224 | tf_op jit(solution)/shard_map/while/body/eval_jaxpr/ppermute | solution.py:13
  568.2 20.7 %collective-permute-start.2 = (f32[2,128,2]{1,2,0:T(2,128)S(1)}, f32[2,128,2]{1,2,0:T(2,128)S(1)}, u32[]{:S(2)}, u32[]{:S(2)}) collective-permute-start(f32[2,128,2]{1,2,0:T(2,128)S(1)} %get-tuple-element.1410), channel_id=1, source_target_pairs={{8,0},{16,8},{24,16},{32,24},{40,32},{48,40},{56,48},{64,56},{72,6... | collective-permute-start | bytes 6152 | tf_op jit(solution)/shard_map/while/body/eval_jaxpr/ppermute | solution.py:13
  589.6 37.1 %collective-permute-start.1 = (bf16[2,128,256]{2,1,0:T(8,128)(2,1)S(1)}, bf16[2,128,256]{2,1,0:T(8,128)(2,1)S(1)}, u32[]{:S(2)}, u32[]{:S(2)}) collective-permute-start(bf16[2,128,256]{2,1,0:T(8,128)(2,1)S(1)} %get-tuple-element.1409), channel_id=1, source_target_pairs={{8,0},{16,8},{24,16},{32,24},{40,32},{48,40},{56,48},{64,56},{72,6... | collective-permute-start | bytes 393224 | tf_op jit(solution)/shard_map/while/body/eval_jaxpr/ppermute | solution.py:13
  590.9 35.8 %collective-permute-start.2 = (f32[2,128,2]{1,2,0:T(2,128)S(1)}, f32[2,128,2]{1,2,0:T(2,128)S(1)}, u32[]{:S(2)}, u32[]{:S(2)}) collective-permute-start(f32[2,128,2]{1,2,0:T(2,128)S(1)} %get-tuple-element.1410), channel_id=1, source_target_pairs={{8,0},{16,8},{24,16},{32,24},{40,32},{48,40},{56,48},{64,56},{72,6... | collective-permute-start | bytes 6152 | tf_op jit(solution)/shard_map/while/body/eval_jaxpr/ppermute | solution.py:13
  627.3 17.1 collective-permute-start.1
  628.6 15.8 collective-permute-start.2
  645.1 15.5 collective-permute-start.1
  646.4 14.2 collective-permute-start.2
  661.3 20.6 %collective-permute-start.1 = (bf16[2,128,256]{2,1,0:T(8,128)(2,1)S(1)}, bf16[2,128,256]{2,1,0:T(8,128)(2,1)S(1)}, u32[]{:S(2)}, u32[]{:S(2)}) collective-permute-start(bf16[2,128,256]{2,1,0:T(8,128)(2,1)S(1)} %get-tuple-element.1409), channel_id=1, source_target_pairs={{8,0},{16,8},{24,16},{32,24},{40,32},{48,40},{56,48},{64,56},{72,6... | collective-permute-start | bytes 393224 | tf_op jit(solution)/shard_map/while/body/eval_jaxpr/ppermute | solution.py:13
  662.6 19.3 %collective-permute-start.2 = (f32[2,128,2]{1,2,0:T(2,128)S(1)}, f32[2,128,2]{1,2,0:T(2,128)S(1)}, u32[]{:S(2)}, u32[]{:S(2)}) collective-permute-start(f32[2,128,2]{1,2,0:T(2,128)S(1)} %get-tuple-element.1410), channel_id=1, source_target_pairs={{8,0},{16,8},{24,16},{32,24},{40,32},{48,40},{56,48},{64,56},{72,6... | collective-permute-start | bytes 6152 | tf_op jit(solution)/shard_map/while/body/eval_jaxpr/ppermute | solution.py:13
  682.6 17.1 collective-permute-start.1
  683.9 15.8 collective-permute-start.2
  700.3 15.5 collective-permute-start.1
  701.6 14.2 collective-permute-start.2
  716.6 20.7 %collective-permute-start.1 = (bf16[2,128,256]{2,1,0:T(8,128)(2,1)S(1)}, bf16[2,128,256]{2,1,0:T(8,128)(2,1)S(1)}, u32[]{:S(2)}, u32[]{:S(2)}) collective-permute-start(bf16[2,128,256]{2,1,0:T(8,128)(2,1)S(1)} %get-tuple-element.1409), channel_id=1, source_target_pairs={{8,0},{16,8},{24,16},{32,24},{40,32},{48,40},{56,48},{64,56},{72,6... | collective-permute-start | bytes 393224 | tf_op jit(solution)/shard_map/while/body/eval_jaxpr/ppermute | solution.py:13
  717.8 19.4 %collective-permute-start.2 = (f32[2,128,2]{1,2,0:T(2,128)S(1)}, f32[2,128,2]{1,2,0:T(2,128)S(1)}, u32[]{:S(2)}, u32[]{:S(2)}) collective-permute-start(f32[2,128,2]{1,2,0:T(2,128)S(1)} %get-tuple-element.1410), channel_id=1, source_target_pairs={{8,0},{16,8},{24,16},{32,24},{40,32},{48,40},{56,48},{64,56},{72,6... | collective-permute-start | bytes 6152 | tf_op jit(solution)/shard_map/while/body/eval_jaxpr/ppermute | solution.py:13
  737.9 17.1 collective-permute-start.1
  739.2 15.8 collective-permute-start.2
  755.6 11.3 collective-permute-start.1
  814.1 922.5 %reduce-scatter.5.cloned.1.call-start = ((), (), s32[]{:S(2)}) async-start(), calls=%async_computation.1 | async-start | bytes 663552
  (18 other events, 959.6 us)
Sparse Core Ops, SparseCore 0:
  814.2 919.8 all-reduce.5
Sparse Core Ops, SparseCore 1:
  830.5 120.5 reduce-scatter.4
where the time goes:
time: 1750 us; the launch traced here: 1740 us
  waiting for transfers between devices  1350 us (77%)
  starting transfers between devices  276 us (16%)
  local copies, waits for them, and re-layouts  44.2 us (3%)
  other arithmetic  19.4 us (1%)
    unnamed x4, waiting for transfers between devices  902 us
    ppermute x72, waiting for transfers between devices, shifted(): lax.ppermute(value, axis, [(source, source + steps) for source in range(i...  445 us
    ppermute x72, starting transfers between devices, shifted(): lax.ppermute(value, axis, [(source, source + steps) for source in range(i...  276 us
  transfers between devices with their start and end apart: 74, of which 49 were waited for; matrix products, arithmetic and copies ran while one was open for 1% of the time, Pallas kernels for 0%

commit v1 on v0

v1 whole, which is shorter than its diff:
```python
import jax
import jax.numpy as jnp
from jax import lax
from jax.experimental import pallas as pl
from jax.experimental.pallas import tpu as pltpu
from jax.sharding import Mesh, PartitionSpec as P

QUERY_SCALE = 1.0 / 12.0
SOFT_CAP = 50.0
PLANE = ("y", "x")
LINES = ("zh", "zl")
CHUNK = 128
WIDTH = 128
GROUP = 4
BLOCKS = 16
SPAN = GROUP * CHUNK
NT = (((1,), (1,)), ((), ()))
TN = (((0,), (0,)), ((), ()))
NN = (((1,), (0,)), ((), ()))
F32 = jnp.float32
BF16 = jnp.bfloat16


def dot(left, right, dims):
    return lax.dot_general(left, right, dims, preferred_element_type=F32)


def swapped(value):
    return lax.ppermute(value, LINES, [(a * 4 + b, b * 4 + a) for a in range(4) for b in range(4)])


def partner(value, axis, mask):
    return lax.ppermute(value, axis, [(i, i ^ mask) for i in range(lax.axis_size(axis))])


def gathered(value, axis):
    return [value] + [partner(value, axis, mask) for mask in (1, 2, 3)]


def returned(parts, axis):
    return [parts[0]] + [partner(parts[mask], axis, mask) for mask in (1, 2, 3)]


def exchange(parts, axes):
    return lax.all_to_all(parts, axes, 0, 0, tiled=True)


def spread(value, count, axes):
    return exchange(jnp.broadcast_to(value[None], (count,) + value.shape), axes)


def added(parts):
    return jnp.sum(parts.astype(F32), axis=0)


def query_bounds(place_ref, lengths_ref):
    block, own = place_ref[0], place_ref[1]
    first = block * SPAN
    lane = lax.broadcasted_iota(jnp.int32, (1, CHUNK), 1)
    pos = jnp.concatenate([first + (own ^ slot) * CHUNK + lane for slot in range(GROUP)], axis=1)
    start = jnp.zeros((1, SPAN), jnp.int32)
    end = jnp.int32(0)
    earliest = jnp.int32(0)
    for doc in range(lengths_ref.shape[0]):
        end = end + lengths_ref[doc]
        start = jnp.where(pos >= end, end, start)
        earliest = jnp.where(end <= first, end, earliest)
    return start, pos, lax.div(earliest, SPAN), block + 1


def join_rows(slots, rows_ref):
    for slot in range(GROUP):
        rows_ref[slot * CHUNK:(slot + 1) * CHUNK, :] = slots[slot][...]


def allowed_pairs(place_ref, block, start, pos):
    key_pos = block * SPAN + place_ref[1] * CHUNK + lax.broadcasted_iota(jnp.int32, (CHUNK, SPAN), 0)
    return (key_pos >= start) & (key_pos <= pos)


def weighted(key_rows, query, allowed):
    capped = jnp.tanh(dot(key_rows, query, NT) * (QUERY_SCALE / SOFT_CAP))
    return capped, jnp.where(allowed, jnp.exp(SOFT_CAP * capped), 0.0)


def stats_kernel(place_ref, lengths_ref, kv_ref, slot0, slot1, slot2, slot3, stats_ref, rows_ref):
    join_rows((slot0, slot1, slot2, slot3), rows_ref)
    start, pos, low, high = query_bounds(place_ref, lengths_ref)

    def step(block, carry):
        key_rows = kv_ref[block, :, :WIDTH]
        value_rows = kv_ref[block, :, WIDTH:]
        allowed = allowed_pairs(place_ref, block, start, pos)
        result = []
        for head in range(2):
            query = rows_ref[:, head * WIDTH:(head + 1) * WIDTH]
            grad = rows_ref[:, (2 + head) * WIDTH:(3 + head) * WIDTH]
            _, weights = weighted(key_rows, query, allowed)
            grad_prob = dot(value_rows, grad, NT)
            result.append(carry[2 * head] + jnp.sum(weights, axis=0, keepdims=True))
            result.append(carry[2 * head + 1] + jnp.sum(weights * grad_prob, axis=0, keepdims=True))
        return tuple(result)

    empty = jnp.zeros((1, SPAN), F32)
    totals = lax.fori_loop(low, high, step, (empty,) * 4)
    stats_ref[...] = jnp.concatenate(totals, axis=0)


def grads_kernel(
    place_ref, lengths_ref, stats_ref, kv_ref, slot0, slot1, slot2, slot3, query_ref, kv_out_ref, rows_ref, sums_ref
):
    join_rows((slot0, slot1, slot2, slot3), rows_ref)
    start, pos, low, high = query_bounds(place_ref, lengths_ref)
    own = place_ref[1]
    lanes = [stats_ref[own ^ lane] for lane in range(GROUP)]
    stats = jnp.concatenate(
        [
            sum(lanes[lane][:, (slot ^ lane) * CHUNK:((slot ^ lane) + 1) * CHUNK] for lane in range(GROUP))
            for slot in range(GROUP)
        ],
        axis=1,
    )
    inverse = [1.0 / stats[2 * head:2 * head + 1] for head in range(2)]
    deltas = [stats[2 * head + 1:2 * head + 2] * inverse[head] for head in range(2)]
    sums_ref[...] = jnp.zeros_like(sums_ref)
    kv_out_ref[...] = jnp.zeros_like(kv_out_ref)

    def step(block, carry):
        key_rows = kv_ref[block, :, :WIDTH]
        value_rows = kv_ref[block, :, WIDTH:]
        allowed = allowed_pairs(place_ref, block, start, pos)
        key_sum = jnp.zeros((CHUNK, WIDTH), F32)
        value_sum = jnp.zeros((CHUNK, WIDTH), F32)
        for head in range(2):
            query = rows_ref[:, head * WIDTH:(head + 1) * WIDTH]
            grad = rows_ref[:, (2 + head) * WIDTH:(3 + head) * WIDTH]
            capped, weights = weighted(key_rows, query, allowed)
            probs = weights * inverse[head]
            grad_prob = dot(value_rows, grad, NT)
            slope = (probs * QUERY_SCALE * (grad_prob - deltas[head]) * (1.0 - capped * capped)).astype(BF16)
            key_sum = key_sum + dot(slope, query, NN)
            value_sum = value_sum + dot(probs.astype(BF16), grad, NN)
            sums_ref[head * WIDTH:(head + 1) * WIDTH, :] += dot(key_rows, slope, TN)
        kv_out_ref[block] = jnp.concatenate([key_sum, value_sum], axis=1).astype(BF16)
        return carry

    lax.fori_loop(low, high, step, 0)
    for slot in range(GROUP):
        query_ref[slot] = sums_ref[:, slot * CHUNK:(slot + 1) * CHUNK].astype(BF16)


def term_kernel(place_ref, wq_ref, wk_ref, wv_ref, query_ref, kv_ref, out_ref):
    rows = wq_ref.shape[0] // 8
    key_part = kv_ref[:, :WIDTH].T
    value_part = kv_ref[:, WIDTH:].T
    for side in range(2):
        for line in range(GROUP):
            block = pl.ds(pl.multiple_of(((place_ref[1] ^ line) * 2 + (place_ref[3] ^ (1 - side))) * rows, 32), rows)
            total = dot(wq_ref[block, :], query_ref[...], NN)
            total = total + dot(wk_ref[block, :], key_part, NN)
            total = total + dot(wv_ref[block, :], value_part, NN)
            out_ref[side, line] = total.astype(BF16)


def run_kernel(body, shapes, scratch, flops, scalars, operands):
    smem = pl.BlockSpec(memory_space=pltpu.SMEM)
    vmem = pl.BlockSpec(memory_space=pltpu.VMEM)
    return pl.pallas_call(
        body,
        out_shape=shapes,
        in_specs=[smem] * len(scalars) + [vmem] * len(operands),
        out_specs=jax.tree.map(lambda _: vmem, shapes),
        scratch_shapes=scratch,
        compiler_params=pltpu.CompilerParams(vmem_limit_bytes=40 * 1024 * 1024),
        cost_estimate=pl.CostEstimate(flops=flops, bytes_accessed=4000000, transcendentals=2000000),
    )(*scalars, *operands)


def shards(inputs, queries, keys, values, grad_out, w_query, w_key, w_value, doc_lengths):
    zh, zl, core = lax.axis_index("zh"), lax.axis_index("zl"), lax.axis_index("c")
    place = jnp.stack([lax.axis_index(PLANE), zl, zh, core]).astype(jnp.int32)
    lengths = doc_lengths.astype(jnp.int32)

    packed = swapped(jnp.concatenate([keys, values, queries, grad_out], axis=1))
    features = lax.all_gather(inputs.T, ("zl", "c"), axis=0, tiled=True)
    packed, features = lax.optimization_barrier((packed, features))
    kv_all = spread(packed[:, :2 * WIDTH], BLOCKS, PLANE)
    rows = gathered(packed[:, 2 * WIDTH:], "zl")
    joined = pltpu.VMEM((SPAN, 4 * WIDTH), BF16)
    stats = run_kernel(
        stats_kernel, jax.ShapeDtypeStruct((4, SPAN), F32), [joined], 500000000, (place, lengths), (kv_all, *rows)
    )
    stats_all = spread(stats, GROUP, "zl")
    query_parts, kv_parts = run_kernel(
        grads_kernel,
        (jax.ShapeDtypeStruct((GROUP, 2 * WIDTH, CHUNK), BF16), jax.ShapeDtypeStruct((BLOCKS, CHUNK, 2 * WIDTH), BF16)),
        [joined, pltpu.VMEM((2 * WIDTH, SPAN), F32)],
        1200000000,
        (place, lengths),
        (stats_all, kv_all, *rows),
    )
    kv_parts = exchange(kv_parts, PLANE)
    query_parts = returned([query_parts[slot] for slot in range(GROUP)], "zl")
    grad_query = swapped(sum(part.astype(F32) for part in query_parts).astype(BF16))
    grad_kv = added(kv_parts).astype(BF16)

    grad_kv = swapped(grad_kv)

    weight = dot(features, grad_kv, NN).astype(BF16).reshape(BLOCKS, -1, 2 * WIDTH)
    weight = added(exchange(weight, PLANE)).astype(BF16).reshape(GROUP, -1, 2 * WIDTH)
    weight = added(exchange(weight, "zh"))

    side = jax.ShapeDtypeStruct((2, GROUP, w_query.shape[0] // 8, CHUNK), BF16)
    terms = run_kernel(term_kernel, side, [], 300000000, (place,), (w_query, w_key, w_value, grad_query, grad_kv))
    both = (terms[1].astype(F32) + partner(terms[0], "c", 1).astype(F32)).astype(BF16)
    pieces = returned([both[slot] for slot in range(GROUP)], "zl")
    grad_input = sum(piece.astype(F32) for piece in pieces).T.astype(BF16)
    return grad_input, weight[:, :WIDTH], weight[:, WIDTH:]


def solution(mesh):
    fine = Mesh(mesh.devices.reshape(4, 4, 4, 4, 2), ("y", "x", "zh", "zl", "c"))
    ctx, head = ("y", "x", "zh"), ("zl", "c")
    split = P(ctx, head)
    return jax.shard_map(
        shards,
        mesh=fine,
        in_specs=(split,) * 5 + (P(None, head),) * 3 + (P(),),
        out_specs=(split,) * 3,
        check_vma=False,
    )
```

time: 1750 us -> 161 us (0.09)
  the two profiles are of different devices: /device:TPU:32 before, /device:TPU:2 now
where the time goes in v1:
time: 161 us; the launch traced here: 160 us
  starting transfers between devices  78.9 us (49%)
  blocking collectives  42 us (26%)
  waiting for transfers between devices  24.5 us (15%)
  Pallas kernels  6.17 us (4%)
  other arithmetic  3.37 us (2%)
  local copies, waits for them, and re-layouts  2.44 us (2%)
    ppermute x10, starting transfers between devices, partner(): lax.ppermute(value, axis, [(i, i ^ mask) for i in range(lax.axis_size(axi...  43.5 us
    all_gather x1, blocking collectives, shards(): features = lax.all_gather(inputs.T, ('zl', 'c'), axis=0, tiled=True)  34 us
    all_to_all x4, starting transfers between devices, exchange(): return lax.all_to_all(parts, axes, 0, 0, tiled=True)  33.3 us
    all_to_all x4, waiting for transfers between devices, exchange(): return lax.all_to_all(parts, axes, 0, 0, tiled=True)  17.4 us
    all_to_all x1, blocking collectives, exchange(): return lax.all_to_all(parts, axes, 0, 0, tiled=True)  8.01 us
    ppermute x10, waiting for transfers between devices, partner(): lax.ppermute(value, axis, [(i, i ^ mask) for i in range(lax.axis_size(axi...  7.06 us
    pallas_call x3, Pallas kernels, run_kernel(): pl.pallas_call(body, out_shape=shapes, in_specs=[smem] * len(scalars) + [...  6.17 us
  transfers between devices with their start and end apart: 17, of which 6 were waited for; matrix products, arithmetic and copies ran while one was open for 3% of the time, Pallas kernels for 1%

profile of v1, /device:TPU:2, one launch (start us, length us, event | category | flops | bytes accessed | tf_op | source)
XLA Modules:
  0.0 159.7 jit_solution(5830609307309197817)
XLA Ops:
  0.6 0.9 pad_maximum_fusion
  1.5 0.7 collective-permute-start
  2.2 34.0 %all_gather.3 = bf16[2304,128]{1,0:T(8,128)(2,1)S(1)} all-gather(bf16[288,128]{1,0:T(8,128)(2,1)} %bitcast.38), channel_id=1, replica_groups=mesh['y'=4,'x'=4,'zh'=4,'zl'=4,'c'=2] {'zl','c'}, dimensions={0}, use_global_device_ids=true | all-gather | bytes 663552 | tf_op jit(solution)/shard_map/all_gather | solution.py:185
  36.2 0.0 collective-permute-done
  36.2 1.1 broadcast_in_dim.4
  37.3 0.0 copy-start.3
  37.3 7.6 %all-to-all-start = ((bf16[16,128,256]{2,1,0:T(8,128)(2,1)}), bf16[16,128,256]{2,1,0:T(8,128)(2,1)S(1)}, u32[]{:S(2)}, u32[]{:S(2)}) async-start(bf16[16,128,256]{2,1,0:T(8,128)(2,1)} %broadcast_in_dim.4), calls=%async_computation | async-start | bytes 2097152 | tf_op jit(solution)/shard_map/all_to_all | solution.py:45
  44.9 2.6 %collective-permute-start.3 = (bf16[128,512]{1,0:T(8,128)(2,1)S(1)}, bf16[128,512]{1,0:T(8,128)(2,1)S(1)}, u32[]{:S(2)}, u32[]{:S(2)}) collective-permute-start(bf16[128,512]{1,0:T(8,128)(2,1)S(1)} %slice.43.slot0), channel_id=1, source_target_pairs={{0,6},{2,4},{4,2},{6,0},{1,7},{3,5},{5,3},{7,1},{8,14},{10,12},{12... | collective-permute-start | bytes 393224 | tf_op jit(solution)/shard_map/ppermute | solution.py:33
  47.6 1.9 %collective-permute-start.2 = (bf16[128,512]{1,0:T(8,128)(2,1)S(1)}, bf16[128,512]{1,0:T(8,128)(2,1)S(1)}, u32[]{:S(2)}, u32[]{:S(2)}) collective-permute-start(bf16[128,512]{1,0:T(8,128)(2,1)S(1)} %slice.43.slot0), channel_id=1, source_target_pairs={{0,4},{2,6},{4,0},{6,2},{1,5},{3,7},{5,1},{7,3},{8,12},{10,14},{12... | collective-permute-start | bytes 393224 | tf_op jit(solution)/shard_map/ppermute | solution.py:33
  49.5 5.6 %collective-permute-start.1 = (bf16[128,512]{1,0:T(8,128)(2,1)S(1)}, bf16[128,512]{1,0:T(8,128)(2,1)S(1)}, u32[]{:S(2)}, u32[]{:S(2)}) collective-permute-start(bf16[128,512]{1,0:T(8,128)(2,1)S(1)} %slice.43.slot0), channel_id=1, source_target_pairs={{0,2},{2,0},{4,6},{6,4},{1,3},{3,1},{5,7},{7,5},{8,10},{10,8},{12,... | collective-permute-start | bytes 393224 | tf_op jit(solution)/shard_map/ppermute | solution.py:33
  55.1 0.1 pad_add_fusion.place_ref
  55.2 0.0 collective-permute-done.3.slot3
  55.2 4.4 %collective-permute-done.2.slot2 = bf16[128,512]{1,0:T(8,128)(2,1)S(1)} collective-permute-done((bf16[128,512]{1,0:T(8,128)(2,1)S(1)}, bf16[128,512]{1,0:T(8,128)(2,1)S(1)}, u32[]{:S(2)}, u32[]{:S(2)}) %collective-permute-start.2) | collective-permute-done | bytes 131104 | tf_op jit(solution)/shard_map/ppermute | solution.py:33
  59.6 1.1 collective-permute-done.1.slot1
  60.7 0.6 all-to-all-done.kv_ref
  61.2 0.0 copy-done.3
  61.2 1.4 shard_map.112
  62.6 8.0 %all_to_all.25.stats_ref = f32[4,4,512]{2,1,0:T(4,128)S(1)} all-to-all(f32[4,4,512]{2,1,0:T(4,128)S(1)} %broadcast_in_dim.5), channel_id=1, replica_groups=mesh['y'=4,'x'=4,'zh'=4,'zl'=4,'c'=2] {'zl'}, dimensions={0} | all-to-all | bytes 65536 | tf_op jit(solution)/shard_map/all_to_all | solution.py:45
  70.6 3.5 %shard_map.113 = (bf16[4,256,128]{2,1,0:T(8,128)(2,1)S(1)}, bf16[16,128,256]{2,1,0:T(8,128)(2,1)}) custom-call(s32[4]{0:T(128)S(1)} %pad_add_fusion.place_ref, s32[17]{0:T(128)S(1)} %copy-done.3, f32[4,4,512]{2,1,0:T(4,128)S(1)} %all_to_all.25.stats_ref, bf16[16,128,256]{2,1,0:T(8,128)(2,1)S(1)} %all-to-all-done.kv_ref, bf16[128,512]{1,0:T(8,128)(2,1)S(1)} %slice.43.slot0, ...), custom_call_target="tpu_custom_call" | custom-call | flops 1200000000 | bytes 4000000 | tf_op jit(solution)/shard_map/pallas_call | solution.py:168
  74.1 11.8 %all-to-all-start.2 = ((bf16[16,128,256]{2,1,0:T(8,128)(2,1)}), bf16[16,128,256]{2,1,0:T(8,128)(2,1)S(1)}, u32[]{:S(2)}, u32[]{:S(2)}) async-start(bf16[16,128,256]{2,1,0:T(8,128)(2,1)} %get-tuple-element.9), calls=%async_computation.2 | async-start | bytes 2097152 | tf_op jit(solution)/shard_map/all_to_all | solution.py:45
  86.0 2.6 %collective-permute-start.4 = (bf16[256,128]{1,0:T(8,128)(2,1)S(1)}, bf16[256,128]{1,0:T(8,128)(2,1)S(1)}, u32[]{:S(2)}, u32[]{:S(2)}) collective-permute-start(bf16[256,128]{1,0:T(8,128)(2,1)S(1)} %get-tuple-element.14), channel_id=1, source_target_pairs={{0,2},{2,0},{4,6},{6,4},{1,3},{3,1},{5,7},{7,5},{8,10},{10,8},{12,... | collective-permute-start | bytes 196616 | tf_op jit(solution)/shard_map/ppermute | solution.py:33
  88.6 3.3 %collective-permute-start.6 = (bf16[256,128]{1,0:T(8,128)(2,1)S(1)}, bf16[256,128]{1,0:T(8,128)(2,1)S(1)}, u32[]{:S(2)}, u32[]{:S(2)}) collective-permute-start(bf16[256,128]{1,0:T(8,128)(2,1)S(1)} %get-tuple-element.15), channel_id=1, source_target_pairs={{0,6},{2,4},{4,2},{6,0},{1,7},{3,5},{5,3},{7,1},{8,14},{10,12},{12... | collective-permute-start | bytes 196616 | tf_op jit(solution)/shard_map/ppermute | solution.py:33
  91.9 3.3 %collective-permute-start.5 = (bf16[256,128]{1,0:T(8,128)(2,1)S(1)}, bf16[256,128]{1,0:T(8,128)(2,1)S(1)}, u32[]{:S(2)}, u32[]{:S(2)}) collective-permute-start(bf16[256,128]{1,0:T(8,128)(2,1)S(1)} %get-tuple-element.16), channel_id=1, source_target_pairs={{0,4},{2,6},{4,0},{6,2},{1,5},{3,7},{5,1},{7,3},{8,12},{10,14},{12... | collective-permute-start | bytes 196616 | tf_op jit(solution)/shard_map/ppermute | solution.py:33
  95.2 4.6 %all-to-all-done.2 = bf16[16,128,256]{2,1,0:T(8,128)(2,1)S(1)} async-done(((bf16[16,128,256]{2,1,0:T(8,128)(2,1)}), bf16[16,128,256]{2,1,0:T(8,128)(2,1)S(1)}, u32[]{:S(2)}, u32[]{:S(2)}) %all-to-all-start.2) | async-done | bytes 1048608 | tf_op jit(solution)/shard_map/all_to_all | solution.py:45
  99.8 0.1 reduce_sum.33
  99.9 0.7 collective-permute-start.8
  100.6 0.0 collective-permute-done.4
  100.6 0.0 collective-permute-done.6
  100.6 0.0 collective-permute-done.5
  100.7 0.7 collective-permute-start.7
  101.4 0.0 collective-permute-done.8.kv_ref
  101.4 1.4 convolution_convert_fusion
  102.8 0.0 copy-start
  102.8 0.0 copy-start.1
  102.8 0.0 copy-start.2
  102.8 5.9 %all-to-all-start.3 = ((bf16[16,144,256]{2,1,0:T(8,128)(2,1)}), bf16[16,144,256]{2,1,0:T(8,128)(2,1)}, u32[]{:S(2)}, u32[]{:S(2)}) async-start(bf16[16,144,256]{2,1,0:T(8,128)(2,1)} %bitcast.37), calls=%async_computation.3 | async-start | bytes 2359296 | tf_op jit(solution)/shard_map/all_to_all | solution.py:45
  108.8 0.0 collective-permute-done.7.query_ref
  108.8 0.0 copy-done
  108.8 0.0 copy-done.1
  108.8 0.0 copy-done.2
  108.8 1.3 shard_map.114
  110.1 1.9 %collective-permute-start.9 = (bf16[4,288,128]{2,1,0:T(8,128)(2,1)S(1)}, bf16[4,288,128]{2,1,0:T(8,128)(2,1)S(1)}, u32[]{:S(2)}, u32[]{:S(2)}) collective-permute-start(bf16[4,288,128]{2,1,0:T(8,128)(2,1)S(1)} %slice_bitcast_fusion), channel_id=1, source_target_pairs={{0,1},{1,0},{2,3},{3,2},{4,5},{5,4},{6,7},{7,6},{8,9},{9,8},{10,11... | collective-permute-start | bytes 884744 | tf_op jit(solution)/shard_map/ppermute | solution.py:33
  112.1 1.5 collective-permute-done.9
  113.6 0.1 fusion
  113.7 10.2 %collective-permute-start.10 = (bf16[288,128]{1,0:T(8,128)(2,1)S(1)}, bf16[288,128]{1,0:T(8,128)(2,1)S(1)}, u32[]{:S(2)}, u32[]{:S(2)}) collective-permute-start(bf16[288,128]{1,0:T(8,128)(2,1)S(1)} %get-tuple-element.11), channel_id=1, source_target_pairs={{0,2},{2,0},{4,6},{6,4},{1,3},{3,1},{5,7},{7,5},{8,10},{10,8},{12,... | collective-permute-start | bytes 221192 | tf_op jit(solution)/shard_map/ppermute | solution.py:33
  123.9 9.7 %collective-permute-start.12 = (bf16[288,128]{1,0:T(8,128)(2,1)S(1)}, bf16[288,128]{1,0:T(8,128)(2,1)S(1)}, u32[]{:S(2)}, u32[]{:S(2)}) collective-permute-start(bf16[288,128]{1,0:T(8,128)(2,1)S(1)} %get-tuple-element.12), channel_id=1, source_target_pairs={{0,6},{2,4},{4,2},{6,0},{1,7},{3,5},{5,3},{7,1},{8,14},{10,12},{12... | collective-permute-start | bytes 221192 | tf_op jit(solution)/shard_map/ppermute | solution.py:33
  133.6 2.4 %collective-permute-start.11 = (bf16[288,128]{1,0:T(8,128)(2,1)S(1)}, bf16[288,128]{1,0:T(8,128)(2,1)S(1)}, u32[]{:S(2)}, u32[]{:S(2)}) collective-permute-start(bf16[288,128]{1,0:T(8,128)(2,1)S(1)} %get-tuple-element.13), channel_id=1, source_target_pairs={{0,4},{2,6},{4,0},{6,2},{1,5},{3,7},{5,1},{7,3},{8,12},{10,14},{12... | collective-permute-start | bytes 221192 | tf_op jit(solution)/shard_map/ppermute | solution.py:33
  136.1 0.0 all-to-all-done.3
  136.1 1.4 reduce_sum.34
  137.5 0.6 reshape.21
  138.2 7.9 %all-to-all-start.4 = ((bf16[4,36,256]{2,1,0:T(8,128)(2,1)}), bf16[4,36,256]{2,1,0:T(8,128)(2,1)S(1)}, u32[]{:S(2)}, u32[]{:S(2)}) async-start(bf16[4,36,256]{2,1,0:T(8,128)(2,1)} %reshape.21), calls=%async_computation.4 | async-start | bytes 163840 | tf_op jit(solution)/shard_map/all_to_all | solution.py:45
  146.1 0.0 collective-permute-done.10
  146.1 0.0 collective-permute-done.12
  146.1 0.0 collective-permute-done.11
  146.1 0.7 fusion.7
  146.8 12.2 %all-to-all-done.4 = bf16[4,36,256]{2,1,0:T(8,128)(2,1)S(1)} async-done(((bf16[4,36,256]{2,1,0:T(8,128)(2,1)}), bf16[4,36,256]{2,1,0:T(8,128)(2,1)S(1)}, u32[]{:S(2)}, u32[]{:S(2)}) %all-to-all-start.4) | async-done | bytes 73760 | tf_op jit(solution)/shard_map/all_to_all | solution.py:45
  159.0 0.6 fusion.8
  (8 shorter events, 0.1 us)
Async XLA Ops:
  1.5 34.7 %collective-permute-start = (bf16[128,768]{1,0:T(8,128)(2,1)S(1)}, bf16[128,768]{1,0:T(8,128)(2,1)S(1)}, u32[]{:S(2)}, u32[]{:S(2)}) collective-permute-start(bf16[128,768]{1,0:T(8,128)(2,1)S(1)} %pad_maximum_fusion), channel_id=1, source_target_pairs={{0,0},{2,8},{4,16},{6,24},{8,2},{10,10},{12,18},{14,26},{16,4},{18... | collective-permute-start | bytes 589832 | tf_op jit(solution)/shard_map/ppermute | solution.py:29
  37.3 23.9 %copy-start.3 = (s32[17]{0:T(128)S(1)}, s32[17]{0:T(128)}, u32[]{:S(2)}) copy-start(s32[17]{0:T(128)} %lengths_ref.3) | copy-start | bytes 208
  37.3 23.9 %all-to-all-start = ((bf16[16,128,256]{2,1,0:T(8,128)(2,1)}), bf16[16,128,256]{2,1,0:T(8,128)(2,1)S(1)}, u32[]{:S(2)}, u32[]{:S(2)}) async-start(bf16[16,128,256]{2,1,0:T(8,128)(2,1)} %broadcast_in_dim.4), calls=%async_computation | async-start | bytes 2097152 | tf_op jit(solution)/shard_map/all_to_all | solution.py:45
  44.9 10.2 %collective-permute-start.3 = (bf16[128,512]{1,0:T(8,128)(2,1)S(1)}, bf16[128,512]{1,0:T(8,128)(2,1)S(1)}, u32[]{:S(2)}, u32[]{:S(2)}) collective-permute-start(bf16[128,512]{1,0:T(8,128)(2,1)S(1)} %slice.43.slot0), channel_id=1, source_target_pairs={{0,6},{2,4},{4,2},{6,0},{1,7},{3,5},{5,3},{7,1},{8,14},{10,12},{12... | collective-permute-start | bytes 393224 | tf_op jit(solution)/shard_map/ppermute | solution.py:33
  47.6 12.0 %collective-permute-start.2 = (bf16[128,512]{1,0:T(8,128)(2,1)S(1)}, bf16[128,512]{1,0:T(8,128)(2,1)S(1)}, u32[]{:S(2)}, u32[]{:S(2)}) collective-permute-start(bf16[128,512]{1,0:T(8,128)(2,1)S(1)} %slice.43.slot0), channel_id=1, source_target_pairs={{0,4},{2,6},{4,0},{6,2},{1,5},{3,7},{5,1},{7,3},{8,12},{10,14},{12... | collective-permute-start | bytes 393224 | tf_op jit(solution)/shard_map/ppermute | solution.py:33
  49.5 11.1 %collective-permute-start.1 = (bf16[128,512]{1,0:T(8,128)(2,1)S(1)}, bf16[128,512]{1,0:T(8,128)(2,1)S(1)}, u32[]{:S(2)}, u32[]{:S(2)}) collective-permute-start(bf16[128,512]{1,0:T(8,128)(2,1)S(1)} %slice.43.slot0), channel_id=1, source_target_pairs={{0,2},{2,0},{4,6},{6,4},{1,3},{3,1},{5,7},{7,5},{8,10},{10,8},{12,... | collective-permute-start | bytes 393224 | tf_op jit(solution)/shard_map/ppermute | solution.py:33
  74.1 25.7 %all-to-all-start.2 = ((bf16[16,128,256]{2,1,0:T(8,128)(2,1)}), bf16[16,128,256]{2,1,0:T(8,128)(2,1)S(1)}, u32[]{:S(2)}, u32[]{:S(2)}) async-start(bf16[16,128,256]{2,1,0:T(8,128)(2,1)} %get-tuple-element.9), calls=%async_computation.2 | async-start | bytes 2097152 | tf_op jit(solution)/shard_map/all_to_all | solution.py:45
  86.0 14.6 %collective-permute-start.4 = (bf16[256,128]{1,0:T(8,128)(2,1)S(1)}, bf16[256,128]{1,0:T(8,128)(2,1)S(1)}, u32[]{:S(2)}, u32[]{:S(2)}) collective-permute-start(bf16[256,128]{1,0:T(8,128)(2,1)S(1)} %get-tuple-element.14), channel_id=1, source_target_pairs={{0,2},{2,0},{4,6},{6,4},{1,3},{3,1},{5,7},{7,5},{8,10},{10,8},{12,... | collective-permute-start | bytes 196616 | tf_op jit(solution)/shard_map/ppermute | solution.py:33
  88.6 12.0 %collective-permute-start.6 = (bf16[256,128]{1,0:T(8,128)(2,1)S(1)}, bf16[256,128]{1,0:T(8,128)(2,1)S(1)}, u32[]{:S(2)}, u32[]{:S(2)}) collective-permute-start(bf16[256,128]{1,0:T(8,128)(2,1)S(1)} %get-tuple-element.15), channel_id=1, source_target_pairs={{0,6},{2,4},{4,2},{6,0},{1,7},{3,5},{5,3},{7,1},{8,14},{10,12},{12... | collective-permute-start | bytes 196616 | tf_op jit(solution)/shard_map/ppermute | solution.py:33
  91.9 8.7 %collective-permute-start.5 = (bf16[256,128]{1,0:T(8,128)(2,1)S(1)}, bf16[256,128]{1,0:T(8,128)(2,1)S(1)}, u32[]{:S(2)}, u32[]{:S(2)}) collective-permute-start(bf16[256,128]{1,0:T(8,128)(2,1)S(1)} %get-tuple-element.16), channel_id=1, source_target_pairs={{0,4},{2,6},{4,0},{6,2},{1,5},{3,7},{5,1},{7,3},{8,12},{10,14},{12... | collective-permute-start | bytes 196616 | tf_op jit(solution)/shard_map/ppermute | solution.py:33
  99.9 1.4 collective-permute-start.8
  100.7 8.1 %collective-permute-start.7 = (bf16[256,128]{1,0:T(8,128)(2,1)S(1)}, bf16[256,128]{1,0:T(8,128)(2,1)S(1)}, u32[]{:S(2)}, u32[]{:S(2)}) collective-permute-start(bf16[256,128]{1,0:T(8,128)(2,1)S(1)} %fusion.6), channel_id=1, source_target_pairs={{0,0},{2,8},{4,16},{6,24},{8,2},{10,10},{12,18},{14,26},{16,4},{18... | collective-permute-start | bytes 196616 | tf_op jit(solution)/shard_map/ppermute | solution.py:29
  102.8 5.9 %copy-start = (bf16[2304,256]{1,0:T(8,128)(2,1)S(1)}, bf16[2304,256]{1,0:T(8,128)(2,1)}, u32[]{:S(2)}) copy-start(bf16[2304,256]{1,0:T(8,128)(2,1)} %wq_ref.1) | copy-start | bytes 3538948
  102.8 5.9 %copy-start.1 = (bf16[2304,128]{1,0:T(8,128)(2,1)S(1)}, bf16[2304,128]{1,0:T(8,128)(2,1)}, u32[]{:S(2)}) copy-start(bf16[2304,128]{1,0:T(8,128)(2,1)} %wk_ref.1) | copy-start | bytes 1769476
  102.8 6.0 %copy-start.2 = (bf16[2304,128]{1,0:T(8,128)(2,1)S(1)}, bf16[2304,128]{1,0:T(8,128)(2,1)}, u32[]{:S(2)}) copy-start(bf16[2304,128]{1,0:T(8,128)(2,1)} %wv_ref.1) | copy-start | bytes 1769476
  102.8 33.2 %all-to-all-start.3 = ((bf16[16,144,256]{2,1,0:T(8,128)(2,1)}), bf16[16,144,256]{2,1,0:T(8,128)(2,1)}, u32[]{:S(2)}, u32[]{:S(2)}) async-start(bf16[16,144,256]{2,1,0:T(8,128)(2,1)} %bitcast.37), calls=%async_computation.3 | async-start | bytes 2359296 | tf_op jit(solution)/shard_map/all_to_all | solution.py:45
  110.1 3.5 %collective-permute-start.9 = (bf16[4,288,128]{2,1,0:T(8,128)(2,1)S(1)}, bf16[4,288,128]{2,1,0:T(8,128)(2,1)S(1)}, u32[]{:S(2)}, u32[]{:S(2)}) collective-permute-start(bf16[4,288,128]{2,1,0:T(8,128)(2,1)S(1)} %slice_bitcast_fusion), channel_id=1, source_target_pairs={{0,1},{1,0},{2,3},{3,2},{4,5},{5,4},{6,7},{7,6},{8,9},{9,8},{10,11... | collective-permute-start | bytes 884744 | tf_op jit(solution)/shard_map/ppermute | solution.py:33
  113.7 32.4 %collective-permute-start.10 = (bf16[288,128]{1,0:T(8,128)(2,1)S(1)}, bf16[288,128]{1,0:T(8,128)(2,1)S(1)}, u32[]{:S(2)}, u32[]{:S(2)}) collective-permute-start(bf16[288,128]{1,0:T(8,128)(2,1)S(1)} %get-tuple-element.11), channel_id=1, source_target_pairs={{0,2},{2,0},{4,6},{6,4},{1,3},{3,1},{5,7},{7,5},{8,10},{10,8},{12,... | collective-permute-start | bytes 221192 | tf_op jit(solution)/shard_map/ppermute | solution.py:33
  123.9 22.2 %collective-permute-start.12 = (bf16[288,128]{1,0:T(8,128)(2,1)S(1)}, bf16[288,128]{1,0:T(8,128)(2,1)S(1)}, u32[]{:S(2)}, u32[]{:S(2)}) collective-permute-start(bf16[288,128]{1,0:T(8,128)(2,1)S(1)} %get-tuple-element.12), channel_id=1, source_target_pairs={{0,6},{2,4},{4,2},{6,0},{1,7},{3,5},{5,3},{7,1},{8,14},{10,12},{12... | collective-permute-start | bytes 221192 | tf_op jit(solution)/shard_map/ppermute | solution.py:33
  133.6 12.5 %collective-permute-start.11 = (bf16[288,128]{1,0:T(8,128)(2,1)S(1)}, bf16[288,128]{1,0:T(8,128)(2,1)S(1)}, u32[]{:S(2)}, u32[]{:S(2)}) collective-permute-start(bf16[288,128]{1,0:T(8,128)(2,1)S(1)} %get-tuple-element.13), channel_id=1, source_target_pairs={{0,4},{2,6},{4,0},{6,2},{1,5},{3,7},{5,1},{7,3},{8,12},{10,14},{12... | collective-permute-start | bytes 221192 | tf_op jit(solution)/shard_map/ppermute | solution.py:33
  138.2 20.9 %all-to-all-start.4 = ((bf16[4,36,256]{2,1,0:T(8,128)(2,1)}), bf16[4,36,256]{2,1,0:T(8,128)(2,1)S(1)}, u32[]{:S(2)}, u32[]{:S(2)}) async-start(bf16[4,36,256]{2,1,0:T(8,128)(2,1)} %reshape.21), calls=%async_computation.4 | async-start | bytes 163840 | tf_op jit(solution)/shard_map/all_to_all | solution.py:45

commit v2 on v1

--- a/solution.py
+++ b/solution.py
@@ -14,6 +14,8 @@
 GROUP = 4
 BLOCKS = 16
 SPAN = GROUP * CHUNK
+PAIR = 2
+TILE = 256
 NT = (((1,), (1,)), ((), ()))
 TN = (((0,), (0,)), ((), ()))
 NN = (((1,), (0,)), ((), ()))
@@ -65,7 +67,7 @@
         end = end + lengths_ref[doc]
         start = jnp.where(pos >= end, end, start)
         earliest = jnp.where(end <= first, end, earliest)
-    return start, pos, lax.div(earliest, SPAN), block + 1
+    return start, pos, lax.div(earliest, PAIR * SPAN), lax.div(block, PAIR) + 1
 
 
 def join_rows(slots, rows_ref):
@@ -74,7 +76,8 @@
 
 
 def allowed_pairs(place_ref, block, start, pos):
-    key_pos = block * SPAN + place_ref[1] * CHUNK + lax.broadcasted_iota(jnp.int32, (CHUNK, SPAN), 0)
+    row = lax.broadcasted_iota(jnp.int32, (PAIR * CHUNK, TILE), 0)
+    key_pos = (block * PAIR) * SPAN + place_ref[1] * CHUNK + row + jnp.where(row >= CHUNK, SPAN - CHUNK, 0)
     return (key_pos >= start) & (key_pos <= pos)
 
 
@@ -88,18 +91,19 @@
     start, pos, low, high = query_bounds(place_ref, lengths_ref)
 
     def step(block, carry):
-        key_rows = kv_ref[block, :, :WIDTH]
-        value_rows = kv_ref[block, :, WIDTH:]
-        allowed = allowed_pairs(place_ref, block, start, pos)
-        result = []
-        for head in range(2):
-            query = rows_ref[:, head * WIDTH:(head + 1) * WIDTH]
-            grad = rows_ref[:, (2 + head) * WIDTH:(3 + head) * WIDTH]
-            _, weights = weighted(key_rows, query, allowed)
-            grad_prob = dot(value_rows, grad, NT)
-            result.append(carry[2 * head] + jnp.sum(weights, axis=0, keepdims=True))
-            result.append(carry[2 * head + 1] + jnp.sum(weights * grad_prob, axis=0, keepdims=True))
-        return tuple(result)
+        kv_rows = kv_ref[pl.ds(block * PAIR, PAIR)].reshape(PAIR * CHUNK, 2 * WIDTH)
+        sums = [[] for _ in range(4)]
+        for first in range(0, SPAN, TILE):
+            part = slice(first, first + TILE)
+            allowed = allowed_pairs(place_ref, block, start[:, part], pos[:, part])
+            for head in range(2):
+                query = rows_ref[part, head * WIDTH:(head + 1) * WIDTH]
+                grad = rows_ref[part, (2 + head) * WIDTH:(3 + head) * WIDTH]
+                _, weights = weighted(kv_rows[:, :WIDTH], query, allowed)
+                grad_prob = dot(kv_rows[:, WIDTH:], grad, NT)
+                sums[2 * head].append(jnp.sum(weights, axis=0, keepdims=True))
+                sums[2 * head + 1].append(jnp.sum(weights * grad_prob, axis=0, keepdims=True))
+        return tuple(total + jnp.concatenate(parts, axis=1) for total, parts in zip(carry, sums))
 
     empty = jnp.zeros((1, SPAN), F32)
     totals = lax.fori_loop(low, high, step, (empty,) * 4)
@@ -126,22 +130,26 @@
     kv_out_ref[...] = jnp.zeros_like(kv_out_ref)
 
     def step(block, carry):
-        key_rows = kv_ref[block, :, :WIDTH]
-        value_rows = kv_ref[block, :, WIDTH:]
-        allowed = allowed_pairs(place_ref, block, start, pos)
-        key_sum = jnp.zeros((CHUNK, WIDTH), F32)
-        value_sum = jnp.zeros((CHUNK, WIDTH), F32)
-        for head in range(2):
-            query = rows_ref[:, head * WIDTH:(head + 1) * WIDTH]
-            grad = rows_ref[:, (2 + head) * WIDTH:(3 + head) * WIDTH]
-            capped, weights = weighted(key_rows, query, allowed)
-            probs = weights * inverse[head]
-            grad_prob = dot(value_rows, grad, NT)
-            slope = (probs * QUERY_SCALE * (grad_prob - deltas[head]) * (1.0 - capped * capped)).astype(BF16)
-            key_sum = key_sum + dot(slope, query, NN)
-            value_sum = value_sum + dot(probs.astype(BF16), grad, NN)
-            sums_ref[head * WIDTH:(head + 1) * WIDTH, :] += dot(key_rows, slope, TN)
-        kv_out_ref[block] = jnp.concatenate([key_sum, value_sum], axis=1).astype(BF16)
+        kv_rows = kv_ref[pl.ds(block * PAIR, PAIR)].reshape(PAIR * CHUNK, 2 * WIDTH)
+        key_rows = kv_rows[:, :WIDTH]
+        key_sum = jnp.zeros((PAIR * CHUNK, WIDTH), F32)
+        value_sum = jnp.zeros((PAIR * CHUNK, WIDTH), F32)
+        for first in range(0, SPAN, TILE):
+            part = slice(first, first + TILE)
+            allowed = allowed_pairs(place_ref, block, start[:, part], pos[:, part])
+            for head in range(2):
+                query = rows_ref[part, head * WIDTH:(head + 1) * WIDTH]
+                grad = rows_ref[part, (2 + head) * WIDTH:(3 + head) * WIDTH]
+                capped, weights = weighted(key_rows, query, allowed)
+                probs = weights * inverse[head][:, part]
+                grad_prob = dot(kv_rows[:, WIDTH:], grad, NT)
+                slope = probs * (grad_prob - deltas[head][:, part]) * (QUERY_SCALE - QUERY_SCALE * capped * capped)
+                slope = slope.astype(BF16)
+                key_sum = key_sum + dot(slope, query, NN)
+                value_sum = value_sum + dot(probs.astype(BF16), grad, NN)
+                sums_ref[head * WIDTH:(head + 1) * WIDTH, part] += dot(key_rows, slope, TN)
+        result = jnp.concatenate([key_sum, value_sum], axis=1).astype(BF16)
+        kv_out_ref[pl.ds(block * PAIR, PAIR)] = result.reshape(PAIR, CHUNK, 2 * WIDTH)
         return carry
 
     lax.fori_loop(low, high, step, 0)

time: 161 us -> 161 us (level)
  no operation moved by 1% of the time
where the time goes in v2:
time: 161 us; the launch traced here: 160 us
  starting transfers between devices  79.8 us (50%)
  blocking collectives  42 us (26%)
  waiting for transfers between devices  24.4 us (15%)
  Pallas kernels  5.5 us (3%)
  other arithmetic  3.37 us (2%)
  local copies, waits for them, and re-layouts  2.44 us (2%)
    ppermute x10, starting transfers between devices, partner(): lax.ppermute(value, axis, [(i, i ^ mask) for i in range(lax.axis_size(axi...  43.5 us
    all_to_all x4, starting transfers between devices, exchange(): return lax.all_to_all(parts, axes, 0, 0, tiled=True)  34.2 us
    all_gather x1, blocking collectives, shards(): features = lax.all_gather(inputs.T, ('zl', 'c'), axis=0, tiled=True)  34 us
    all_to_all x4, waiting for transfers between devices, exchange(): return lax.all_to_all(parts, axes, 0, 0, tiled=True)  17.4 us
    all_to_all x1, blocking collectives, exchange(): return lax.all_to_all(parts, axes, 0, 0, tiled=True)  8.01 us
    ppermute x10, waiting for transfers between devices, partner(): lax.ppermute(value, axis, [(i, i ^ mask) for i in range(lax.axis_size(axi...  7.06 us
    pallas_call x3, Pallas kernels, run_kernel(): pl.pallas_call(body, out_shape=shapes, in_specs=[smem] * len(scalars) + [...  5.5 us
  transfers between devices with their start and end apart: 17, of which 6 were waited for; matrix products, arithmetic and copies ran while one was open for 3% of the time, Pallas kernels for 1%

profile of v2, /device:TPU:2, one launch (start us, length us, event | category | flops | bytes accessed | tf_op | source)
XLA Modules:
  0.0 159.9 jit_solution(11298919506495112549)
XLA Ops:
  0.6 0.9 pad_maximum_fusion
  1.5 0.7 collective-permute-start
  2.2 34.0 %all_gather.3 = bf16[2304,128]{1,0:T(8,128)(2,1)S(1)} all-gather(bf16[288,128]{1,0:T(8,128)(2,1)} %bitcast.38), channel_id=1, replica_groups=mesh['y'=4,'x'=4,'zh'=4,'zl'=4,'c'=2] {'zl','c'}, dimensions={0}, use_global_device_ids=true | all-gather | bytes 663552 | tf_op jit(solution)/shard_map/all_gather | solution.py:193
  36.2 0.0 collective-permute-done
  36.2 1.1 broadcast_in_dim.4
  37.3 0.0 copy-start.3
  37.3 7.6 %all-to-all-start = ((bf16[16,128,256]{2,1,0:T(8,128)(2,1)}), bf16[16,128,256]{2,1,0:T(8,128)(2,1)S(1)}, u32[]{:S(2)}, u32[]{:S(2)}) async-start(bf16[16,128,256]{2,1,0:T(8,128)(2,1)} %broadcast_in_dim.4), calls=%async_computation | async-start | bytes 2097152 | tf_op jit(solution)/shard_map/all_to_all | solution.py:47
  44.9 2.6 %collective-permute-start.3 = (bf16[128,512]{1,0:T(8,128)(2,1)S(1)}, bf16[128,512]{1,0:T(8,128)(2,1)S(1)}, u32[]{:S(2)}, u32[]{:S(2)}) collective-permute-start(bf16[128,512]{1,0:T(8,128)(2,1)S(1)} %slice.43.slot0), channel_id=1, source_target_pairs={{0,6},{2,4},{4,2},{6,0},{1,7},{3,5},{5,3},{7,1},{8,14},{10,12},{12... | collective-permute-start | bytes 393224 | tf_op jit(solution)/shard_map/ppermute | solution.py:35
  47.6 1.9 %collective-permute-start.2 = (bf16[128,512]{1,0:T(8,128)(2,1)S(1)}, bf16[128,512]{1,0:T(8,128)(2,1)S(1)}, u32[]{:S(2)}, u32[]{:S(2)}) collective-permute-start(bf16[128,512]{1,0:T(8,128)(2,1)S(1)} %slice.43.slot0), channel_id=1, source_target_pairs={{0,4},{2,6},{4,0},{6,2},{1,5},{3,7},{5,1},{7,3},{8,12},{10,14},{12... | collective-permute-start | bytes 393224 | tf_op jit(solution)/shard_map/ppermute | solution.py:35
  49.5 5.6 %collective-permute-start.1 = (bf16[128,512]{1,0:T(8,128)(2,1)S(1)}, bf16[128,512]{1,0:T(8,128)(2,1)S(1)}, u32[]{:S(2)}, u32[]{:S(2)}) collective-permute-start(bf16[128,512]{1,0:T(8,128)(2,1)S(1)} %slice.43.slot0), channel_id=1, source_target_pairs={{0,2},{2,0},{4,6},{6,4},{1,3},{3,1},{5,7},{7,5},{8,10},{10,8},{12,... | collective-permute-start | bytes 393224 | tf_op jit(solution)/shard_map/ppermute | solution.py:35
  55.1 0.1 pad_add_fusion.place_ref
  55.2 0.0 collective-permute-done.3.slot3
  55.2 4.4 %collective-permute-done.2.slot2 = bf16[128,512]{1,0:T(8,128)(2,1)S(1)} collective-permute-done((bf16[128,512]{1,0:T(8,128)(2,1)S(1)}, bf16[128,512]{1,0:T(8,128)(2,1)S(1)}, u32[]{:S(2)}, u32[]{:S(2)}) %collective-permute-start.2) | collective-permute-done | bytes 131104 | tf_op jit(solution)/shard_map/ppermute | solution.py:35
  59.6 1.1 collective-permute-done.1.slot1
  60.7 0.6 all-to-all-done.kv_ref
  61.2 0.0 copy-done.3
  61.2 1.2 shard_map.112
  62.5 8.0 %all_to_all.25.stats_ref = f32[4,4,512]{2,1,0:T(4,128)S(1)} all-to-all(f32[4,4,512]{2,1,0:T(4,128)S(1)} %broadcast_in_dim.5), channel_id=1, replica_groups=mesh['y'=4,'x'=4,'zh'=4,'zl'=4,'c'=2] {'zl'}, dimensions={0} | all-to-all | bytes 65536 | tf_op jit(solution)/shard_map/all_to_all | solution.py:47
  70.5 3.0 %shard_map.113 = (bf16[4,256,128]{2,1,0:T(8,128)(2,1)S(1)}, bf16[16,128,256]{2,1,0:T(8,128)(2,1)}) custom-call(s32[4]{0:T(128)S(1)} %pad_add_fusion.place_ref, s32[17]{0:T(128)S(1)} %copy-done.3, f32[4,4,512]{2,1,0:T(4,128)S(1)} %all_to_all.25.stats_ref, bf16[16,128,256]{2,1,0:T(8,128)(2,1)S(1)} %all-to-all-done.kv_ref, bf16[128,512]{1,0:T(8,128)(2,1)S(1)} %slice.43.slot0, ...), custom_call_target="tpu_custom_call" | custom-call | flops 1200000000 | bytes 4000000 | tf_op jit(solution)/shard_map/pallas_call | solution.py:176
  73.5 12.7 %all-to-all-start.2 = ((bf16[16,128,256]{2,1,0:T(8,128)(2,1)}), bf16[16,128,256]{2,1,0:T(8,128)(2,1)S(1)}, u32[]{:S(2)}, u32[]{:S(2)}) async-start(bf16[16,128,256]{2,1,0:T(8,128)(2,1)} %get-tuple-element.9), calls=%async_computation.2 | async-start | bytes 2097152 | tf_op jit(solution)/shard_map/all_to_all | solution.py:47
  86.2 2.7 %collective-permute-start.4 = (bf16[256,128]{1,0:T(8,128)(2,1)S(1)}, bf16[256,128]{1,0:T(8,128)(2,1)S(1)}, u32[]{:S(2)}, u32[]{:S(2)}) collective-permute-start(bf16[256,128]{1,0:T(8,128)(2,1)S(1)} %get-tuple-element.14), channel_id=1, source_target_pairs={{0,2},{2,0},{4,6},{6,4},{1,3},{3,1},{5,7},{7,5},{8,10},{10,8},{12,... | collective-permute-start | bytes 196616 | tf_op jit(solution)/shard_map/ppermute | solution.py:35
  88.9 3.3 %collective-permute-start.6 = (bf16[256,128]{1,0:T(8,128)(2,1)S(1)}, bf16[256,128]{1,0:T(8,128)(2,1)S(1)}, u32[]{:S(2)}, u32[]{:S(2)}) collective-permute-start(bf16[256,128]{1,0:T(8,128)(2,1)S(1)} %get-tuple-element.15), channel_id=1, source_target_pairs={{0,6},{2,4},{4,2},{6,0},{1,7},{3,5},{5,3},{7,1},{8,14},{10,12},{12... | collective-permute-start | bytes 196616 | tf_op jit(solution)/shard_map/ppermute | solution.py:35
  92.1 3.3 %collective-permute-start.5 = (bf16[256,128]{1,0:T(8,128)(2,1)S(1)}, bf16[256,128]{1,0:T(8,128)(2,1)S(1)}, u32[]{:S(2)}, u32[]{:S(2)}) collective-permute-start(bf16[256,128]{1,0:T(8,128)(2,1)S(1)} %get-tuple-element.16), channel_id=1, source_target_pairs={{0,4},{2,6},{4,0},{6,2},{1,5},{3,7},{5,1},{7,3},{8,12},{10,14},{12... | collective-permute-start | bytes 196616 | tf_op jit(solution)/shard_map/ppermute | solution.py:35
  95.4 4.6 %all-to-all-done.2 = bf16[16,128,256]{2,1,0:T(8,128)(2,1)S(1)} async-done(((bf16[16,128,256]{2,1,0:T(8,128)(2,1)}), bf16[16,128,256]{2,1,0:T(8,128)(2,1)S(1)}, u32[]{:S(2)}, u32[]{:S(2)}) %all-to-all-start.2) | async-done | bytes 1048608 | tf_op jit(solution)/shard_map/all_to_all | solution.py:47
  100.0 0.1 reduce_sum.33
  100.2 0.7 collective-permute-start.8
  100.8 0.0 collective-permute-done.4
  100.8 0.0 collective-permute-done.6
  100.9 0.0 collective-permute-done.5
  100.9 0.7 collective-permute-start.7
  101.6 0.0 collective-permute-done.8.kv_ref
  101.6 1.5 convolution_convert_fusion
  103.1 0.0 copy-start
  103.1 0.0 copy-start.1
  103.1 0.0 copy-start.2
  103.1 5.9 %all-to-all-start.3 = ((bf16[16,144,256]{2,1,0:T(8,128)(2,1)}), bf16[16,144,256]{2,1,0:T(8,128)(2,1)}, u32[]{:S(2)}, u32[]{:S(2)}) async-start(bf16[16,144,256]{2,1,0:T(8,128)(2,1)} %bitcast.37), calls=%async_computation.3 | async-start | bytes 2359296 | tf_op jit(solution)/shard_map/all_to_all | solution.py:47
  109.0 0.0 collective-permute-done.7.query_ref
  109.0 0.0 copy-done
  109.0 0.0 copy-done.1
  109.0 0.0 copy-done.2
  109.0 1.3 shard_map.114
  110.4 1.9 %collective-permute-start.9 = (bf16[4,288,128]{2,1,0:T(8,128)(2,1)S(1)}, bf16[4,288,128]{2,1,0:T(8,128)(2,1)S(1)}, u32[]{:S(2)}, u32[]{:S(2)}) collective-permute-start(bf16[4,288,128]{2,1,0:T(8,128)(2,1)S(1)} %slice_bitcast_fusion), channel_id=1, source_target_pairs={{0,1},{1,0},{2,3},{3,2},{4,5},{5,4},{6,7},{7,6},{8,9},{9,8},{10,11... | collective-permute-start | bytes 884744 | tf_op jit(solution)/shard_map/ppermute | solution.py:35
  112.3 1.5 collective-permute-done.9
  113.9 0.1 fusion
  114.0 10.1 %collective-permute-start.10 = (bf16[288,128]{1,0:T(8,128)(2,1)S(1)}, bf16[288,128]{1,0:T(8,128)(2,1)S(1)}, u32[]{:S(2)}, u32[]{:S(2)}) collective-permute-start(bf16[288,128]{1,0:T(8,128)(2,1)S(1)} %get-tuple-element.11), channel_id=1, source_target_pairs={{0,2},{2,0},{4,6},{6,4},{1,3},{3,1},{5,7},{7,5},{8,10},{10,8},{12,... | collective-permute-start | bytes 221192 | tf_op jit(solution)/shard_map/ppermute | solution.py:35
  124.1 9.7 %collective-permute-start.12 = (bf16[288,128]{1,0:T(8,128)(2,1)S(1)}, bf16[288,128]{1,0:T(8,128)(2,1)S(1)}, u32[]{:S(2)}, u32[]{:S(2)}) collective-permute-start(bf16[288,128]{1,0:T(8,128)(2,1)S(1)} %get-tuple-element.12), channel_id=1, source_target_pairs={{0,6},{2,4},{4,2},{6,0},{1,7},{3,5},{5,3},{7,1},{8,14},{10,12},{12... | collective-permute-start | bytes 221192 | tf_op jit(solution)/shard_map/ppermute | solution.py:35
  133.8 2.4 %collective-permute-start.11 = (bf16[288,128]{1,0:T(8,128)(2,1)S(1)}, bf16[288,128]{1,0:T(8,128)(2,1)S(1)}, u32[]{:S(2)}, u32[]{:S(2)}) collective-permute-start(bf16[288,128]{1,0:T(8,128)(2,1)S(1)} %get-tuple-element.13), channel_id=1, source_target_pairs={{0,4},{2,6},{4,0},{6,2},{1,5},{3,7},{5,1},{7,3},{8,12},{10,14},{12... | collective-permute-start | bytes 221192 | tf_op jit(solution)/shard_map/ppermute | solution.py:35
  136.3 0.0 all-to-all-done.3
  136.3 1.4 reduce_sum.34
  137.7 0.6 reshape.21
  138.4 8.0 %all-to-all-start.4 = ((bf16[4,36,256]{2,1,0:T(8,128)(2,1)}), bf16[4,36,256]{2,1,0:T(8,128)(2,1)S(1)}, u32[]{:S(2)}, u32[]{:S(2)}) async-start(bf16[4,36,256]{2,1,0:T(8,128)(2,1)} %reshape.21), calls=%async_computation.4 | async-start | bytes 163840 | tf_op jit(solution)/shard_map/all_to_all | solution.py:47
  146.3 0.0 collective-permute-done.10
  146.3 0.0 collective-permute-done.12
  146.3 0.0 collective-permute-done.11
  146.4 0.7 fusion.7
  147.0 12.2 %all-to-all-done.4 = bf16[4,36,256]{2,1,0:T(8,128)(2,1)S(1)} async-done(((bf16[4,36,256]{2,1,0:T(8,128)(2,1)}), bf16[4,36,256]{2,1,0:T(8,128)(2,1)S(1)}, u32[]{:S(2)}, u32[]{:S(2)}) %all-to-all-start.4) | async-done | bytes 73760 | tf_op jit(solution)/shard_map/all_to_all | solution.py:47
  159.3 0.6 fusion.8
  (8 shorter events, 0.1 us)
Async XLA Ops:
  1.5 34.7 %collective-permute-start = (bf16[128,768]{1,0:T(8,128)(2,1)S(1)}, bf16[128,768]{1,0:T(8,128)(2,1)S(1)}, u32[]{:S(2)}, u32[]{:S(2)}) collective-permute-start(bf16[128,768]{1,0:T(8,128)(2,1)S(1)} %pad_maximum_fusion), channel_id=1, source_target_pairs={{0,0},{2,8},{4,16},{6,24},{8,2},{10,10},{12,18},{14,26},{16,4},{18... | collective-permute-start | bytes 589832 | tf_op jit(solution)/shard_map/ppermute | solution.py:31
  37.3 23.9 %copy-start.3 = (s32[17]{0:T(128)S(1)}, s32[17]{0:T(128)}, u32[]{:S(2)}) copy-start(s32[17]{0:T(128)} %lengths_ref.3) | copy-start | bytes 208
  37.3 23.9 %all-to-all-start = ((bf16[16,128,256]{2,1,0:T(8,128)(2,1)}), bf16[16,128,256]{2,1,0:T(8,128)(2,1)S(1)}, u32[]{:S(2)}, u32[]{:S(2)}) async-start(bf16[16,128,256]{2,1,0:T(8,128)(2,1)} %broadcast_in_dim.4), calls=%async_computation | async-start | bytes 2097152 | tf_op jit(solution)/shard_map/all_to_all | solution.py:47
  44.9 10.2 %collective-permute-start.3 = (bf16[128,512]{1,0:T(8,128)(2,1)S(1)}, bf16[128,512]{1,0:T(8,128)(2,1)S(1)}, u32[]{:S(2)}, u32[]{:S(2)}) collective-permute-start(bf16[128,512]{1,0:T(8,128)(2,1)S(1)} %slice.43.slot0), channel_id=1, source_target_pairs={{0,6},{2,4},{4,2},{6,0},{1,7},{3,5},{5,3},{7,1},{8,14},{10,12},{12... | collective-permute-start | bytes 393224 | tf_op jit(solution)/shard_map/ppermute | solution.py:35
  47.6 12.0 %collective-permute-start.2 = (bf16[128,512]{1,0:T(8,128)(2,1)S(1)}, bf16[128,512]{1,0:T(8,128)(2,1)S(1)}, u32[]{:S(2)}, u32[]{:S(2)}) collective-permute-start(bf16[128,512]{1,0:T(8,128)(2,1)S(1)} %slice.43.slot0), channel_id=1, source_target_pairs={{0,4},{2,6},{4,0},{6,2},{1,5},{3,7},{5,1},{7,3},{8,12},{10,14},{12... | collective-permute-start | bytes 393224 | tf_op jit(solution)/shard_map/ppermute | solution.py:35
  49.5 11.1 %collective-permute-start.1 = (bf16[128,512]{1,0:T(8,128)(2,1)S(1)}, bf16[128,512]{1,0:T(8,128)(2,1)S(1)}, u32[]{:S(2)}, u32[]{:S(2)}) collective-permute-start(bf16[128,512]{1,0:T(8,128)(2,1)S(1)} %slice.43.slot0), channel_id=1, source_target_pairs={{0,2},{2,0},{4,6},{6,4},{1,3},{3,1},{5,7},{7,5},{8,10},{10,8},{12,... | collective-permute-start | bytes 393224 | tf_op jit(solution)/shard_map/ppermute | solution.py:35
  73.5 26.6 %all-to-all-start.2 = ((bf16[16,128,256]{2,1,0:T(8,128)(2,1)}), bf16[16,128,256]{2,1,0:T(8,128)(2,1)S(1)}, u32[]{:S(2)}, u32[]{:S(2)}) async-start(bf16[16,128,256]{2,1,0:T(8,128)(2,1)} %get-tuple-element.9), calls=%async_computation.2 | async-start | bytes 2097152 | tf_op jit(solution)/shard_map/all_to_all | solution.py:47
  86.2 14.6 %collective-permute-start.4 = (bf16[256,128]{1,0:T(8,128)(2,1)S(1)}, bf16[256,128]{1,0:T(8,128)(2,1)S(1)}, u32[]{:S(2)}, u32[]{:S(2)}) collective-permute-start(bf16[256,128]{1,0:T(8,128)(2,1)S(1)} %get-tuple-element.14), channel_id=1, source_target_pairs={{0,2},{2,0},{4,6},{6,4},{1,3},{3,1},{5,7},{7,5},{8,10},{10,8},{12,... | collective-permute-start | bytes 196616 | tf_op jit(solution)/shard_map/ppermute | solution.py:35
  88.9 12.0 %collective-permute-start.6 = (bf16[256,128]{1,0:T(8,128)(2,1)S(1)}, bf16[256,128]{1,0:T(8,128)(2,1)S(1)}, u32[]{:S(2)}, u32[]{:S(2)}) collective-permute-start(bf16[256,128]{1,0:T(8,128)(2,1)S(1)} %get-tuple-element.15), channel_id=1, source_target_pairs={{0,6},{2,4},{4,2},{6,0},{1,7},{3,5},{5,3},{7,1},{8,14},{10,12},{12... | collective-permute-start | bytes 196616 | tf_op jit(solution)/shard_map/ppermute | solution.py:35
  92.1 8.7 %collective-permute-start.5 = (bf16[256,128]{1,0:T(8,128)(2,1)S(1)}, bf16[256,128]{1,0:T(8,128)(2,1)S(1)}, u32[]{:S(2)}, u32[]{:S(2)}) collective-permute-start(bf16[256,128]{1,0:T(8,128)(2,1)S(1)} %get-tuple-element.16), channel_id=1, source_target_pairs={{0,4},{2,6},{4,0},{6,2},{1,5},{3,7},{5,1},{7,3},{8,12},{10,14},{12... | collective-permute-start | bytes 196616 | tf_op jit(solution)/shard_map/ppermute | solution.py:35
  100.2 1.4 collective-permute-start.8
  100.9 8.1 %collective-permute-start.7 = (bf16[256,128]{1,0:T(8,128)(2,1)S(1)}, bf16[256,128]{1,0:T(8,128)(2,1)S(1)}, u32[]{:S(2)}, u32[]{:S(2)}) collective-permute-start(bf16[256,128]{1,0:T(8,128)(2,1)S(1)} %fusion.6), channel_id=1, source_target_pairs={{0,0},{2,8},{4,16},{6,24},{8,2},{10,10},{12,18},{14,26},{16,4},{18... | collective-permute-start | bytes 196616 | tf_op jit(solution)/shard_map/ppermute | solution.py:31
  103.1 5.9 %copy-start = (bf16[2304,256]{1,0:T(8,128)(2,1)S(1)}, bf16[2304,256]{1,0:T(8,128)(2,1)}, u32[]{:S(2)}) copy-start(bf16[2304,256]{1,0:T(8,128)(2,1)} %wq_ref.1) | copy-start | bytes 3538948
  103.1 6.0 %copy-start.1 = (bf16[2304,128]{1,0:T(8,128)(2,1)S(1)}, bf16[2304,128]{1,0:T(8,128)(2,1)}, u32[]{:S(2)}) copy-start(bf16[2304,128]{1,0:T(8,128)(2,1)} %wk_ref.1) | copy-start | bytes 1769476
  103.1 6.0 %copy-start.2 = (bf16[2304,128]{1,0:T(8,128)(2,1)S(1)}, bf16[2304,128]{1,0:T(8,128)(2,1)}, u32[]{:S(2)}) copy-start(bf16[2304,128]{1,0:T(8,128)(2,1)} %wv_ref.1) | copy-start | bytes 1769476
  103.1 33.2 %all-to-all-start.3 = ((bf16[16,144,256]{2,1,0:T(8,128)(2,1)}), bf16[16,144,256]{2,1,0:T(8,128)(2,1)}, u32[]{:S(2)}, u32[]{:S(2)}) async-start(bf16[16,144,256]{2,1,0:T(8,128)(2,1)} %bitcast.37), calls=%async_computation.3 | async-start | bytes 2359296 | tf_op jit(solution)/shard_map/all_to_all | solution.py:47
  110.4 3.5 %collective-permute-start.9 = (bf16[4,288,128]{2,1,0:T(8,128)(2,1)S(1)}, bf16[4,288,128]{2,1,0:T(8,128)(2,1)S(1)}, u32[]{:S(2)}, u32[]{:S(2)}) collective-permute-start(bf16[4,288,128]{2,1,0:T(8,128)(2,1)S(1)} %slice_bitcast_fusion), channel_id=1, source_target_pairs={{0,1},{1,0},{2,3},{3,2},{4,5},{5,4},{6,7},{7,6},{8,9},{9,8},{10,11... | collective-permute-start | bytes 884744 | tf_op jit(solution)/shard_map/ppermute | solution.py:35
  114.0 32.4 %collective-permute-start.10 = (bf16[288,128]{1,0:T(8,128)(2,1)S(1)}, bf16[288,128]{1,0:T(8,128)(2,1)S(1)}, u32[]{:S(2)}, u32[]{:S(2)}) collective-permute-start(bf16[288,128]{1,0:T(8,128)(2,1)S(1)} %get-tuple-element.11), channel_id=1, source_target_pairs={{0,2},{2,0},{4,6},{6,4},{1,3},{3,1},{5,7},{7,5},{8,10},{10,8},{12,... | collective-permute-start | bytes 221192 | tf_op jit(solution)/shard_map/ppermute | solution.py:35
  124.1 22.2 %collective-permute-start.12 = (bf16[288,128]{1,0:T(8,128)(2,1)S(1)}, bf16[288,128]{1,0:T(8,128)(2,1)S(1)}, u32[]{:S(2)}, u32[]{:S(2)}) collective-permute-start(bf16[288,128]{1,0:T(8,128)(2,1)S(1)} %get-tuple-element.12), channel_id=1, source_target_pairs={{0,6},{2,4},{4,2},{6,0},{1,7},{3,5},{5,3},{7,1},{8,14},{10,12},{12... | collective-permute-start | bytes 221192 | tf_op jit(solution)/shard_map/ppermute | solution.py:35
  133.8 12.5 %collective-permute-start.11 = (bf16[288,128]{1,0:T(8,128)(2,1)S(1)}, bf16[288,128]{1,0:T(8,128)(2,1)S(1)}, u32[]{:S(2)}, u32[]{:S(2)}) collective-permute-start(bf16[288,128]{1,0:T(8,128)(2,1)S(1)} %get-tuple-element.13), channel_id=1, source_target_pairs={{0,4},{2,6},{4,0},{6,2},{1,5},{3,7},{5,1},{7,3},{8,12},{10,14},{12... | collective-permute-start | bytes 221192 | tf_op jit(solution)/shard_map/ppermute | solution.py:35
  138.4 20.9 %all-to-all-start.4 = ((bf16[4,36,256]{2,1,0:T(8,128)(2,1)}), bf16[4,36,256]{2,1,0:T(8,128)(2,1)S(1)}, u32[]{:S(2)}, u32[]{:S(2)}) async-start(bf16[4,36,256]{2,1,0:T(8,128)(2,1)} %reshape.21), calls=%async_computation.4 | async-start | bytes 163840 | tf_op jit(solution)/shard_map/all_to_all | solution.py:47

commit v3 on v2

--- a/solution.py
+++ b/solution.py
@@ -7,6 +7,7 @@
 
 QUERY_SCALE = 1.0 / 12.0
 SOFT_CAP = 50.0
+LOG2_E = 1.4426950408889634
 PLANE = ("y", "x")
 LINES = ("zh", "zl")
 CHUNK = 128
@@ -83,7 +84,7 @@
 
 def weighted(key_rows, query, allowed):
     capped = jnp.tanh(dot(key_rows, query, NT) * (QUERY_SCALE / SOFT_CAP))
-    return capped, jnp.where(allowed, jnp.exp(SOFT_CAP * capped), 0.0)
+    return capped, jnp.where(allowed, jnp.exp2(SOFT_CAP * LOG2_E * capped), 0.0)
 
 
 def stats_kernel(place_ref, lengths_ref, kv_ref, slot0, slot1, slot2, slot3, stats_ref, rows_ref):
@@ -127,7 +128,13 @@
     inverse = [1.0 / stats[2 * head:2 * head + 1] for head in range(2)]
     deltas = [stats[2 * head + 1:2 * head + 2] * inverse[head] for head in range(2)]
     sums_ref[...] = jnp.zeros_like(sums_ref)
-    kv_out_ref[...] = jnp.zeros_like(kv_out_ref)
+
+    def clear(block, carry):
+        kv_out_ref[pl.ds(block * PAIR, PAIR)] = jnp.zeros((PAIR, CHUNK, 2 * WIDTH), BF16)
+        return carry
+
+    lax.fori_loop(0, low, clear, 0)
+    lax.fori_loop(high, BLOCKS // PAIR, clear, 0)
 
     def step(block, carry):
         kv_rows = kv_ref[pl.ds(block * PAIR, PAIR)].reshape(PAIR * CHUNK, 2 * WIDTH)
@@ -179,7 +186,7 @@
         in_specs=[smem] * len(scalars) + [vmem] * len(operands),
         out_specs=jax.tree.map(lambda _: vmem, shapes),
         scratch_shapes=scratch,
-        compiler_params=pltpu.CompilerParams(vmem_limit_bytes=40 * 1024 * 1024),
+        compiler_params=pltpu.CompilerParams(vmem_limit_bytes=16 * 1024 * 1024),
         cost_estimate=pl.CostEstimate(flops=flops, bytes_accessed=4000000, transcendentals=2000000),
     )(*scalars, *operands)
 

time: 161 us -> 160 us (level)
  no operation moved by 1% of the time
where the time goes in v3:
time: 160 us; the launch traced here: 158 us
  starting transfers between devices  78.4 us (49%)
  blocking collectives  42 us (26%)
  waiting for transfers between devices  24.5 us (15%)
  Pallas kernels  5.47 us (3%)
  other arithmetic  3.37 us (2%)
  local copies, waits for them, and re-layouts  2.44 us (2%)
    ppermute x10, starting transfers between devices, partner(): lax.ppermute(value, axis, [(i, i ^ mask) for i in range(lax.axis_size(axi...  43.5 us
    all_gather x1, blocking collectives, shards(): features = lax.all_gather(inputs.T, ('zl', 'c'), axis=0, tiled=True)  34 us
    all_to_all x4, starting transfers between devices, exchange(): return lax.all_to_all(parts, axes, 0, 0, tiled=True)  32.8 us
    all_to_all x4, waiting for transfers between devices, exchange(): return lax.all_to_all(parts, axes, 0, 0, tiled=True)  17.4 us
    all_to_all x1, blocking collectives, exchange(): return lax.all_to_all(parts, axes, 0, 0, tiled=True)  8.01 us
    ppermute x10, waiting for transfers between devices, partner(): lax.ppermute(value, axis, [(i, i ^ mask) for i in range(lax.axis_size(axi...  7.06 us
    pallas_call x3, Pallas kernels, run_kernel(): pl.pallas_call(body, out_shape=shapes, in_specs=[smem] * len(scalars) + [...  5.47 us
  transfers between devices with their start and end apart: 17, of which 6 were waited for; matrix products, arithmetic and copies ran while one was open for 3% of the time, Pallas kernels for 1%

profile of v3, /device:TPU:2, one launch (start us, length us, event | category | flops | bytes accessed | tf_op | source)
XLA Modules:
  0.0 158.5 jit_solution(9223705784385781321)
XLA Ops:
  0.6 0.9 pad_maximum_fusion
  1.5 0.7 collective-permute-start
  2.2 34.0 %all_gather.3 = bf16[2304,128]{1,0:T(8,128)(2,1)S(1)} all-gather(bf16[288,128]{1,0:T(8,128)(2,1)} %bitcast.38), channel_id=1, replica_groups=mesh['y'=4,'x'=4,'zh'=4,'zl'=4,'c'=2] {'zl','c'}, dimensions={0}, use_global_device_ids=true | all-gather | bytes 663552 | tf_op jit(solution)/shard_map/all_gather | solution.py:200
  36.2 0.0 collective-permute-done
  36.2 1.1 broadcast_in_dim.4
  37.3 0.0 copy-start.3
  37.3 7.6 %all-to-all-start = ((bf16[16,128,256]{2,1,0:T(8,128)(2,1)}), bf16[16,128,256]{2,1,0:T(8,128)(2,1)S(1)}, u32[]{:S(2)}, u32[]{:S(2)}) async-start(bf16[16,128,256]{2,1,0:T(8,128)(2,1)} %broadcast_in_dim.4), calls=%async_computation | async-start | bytes 2097152 | tf_op jit(solution)/shard_map/all_to_all | solution.py:48
  44.9 2.6 %collective-permute-start.3 = (bf16[128,512]{1,0:T(8,128)(2,1)S(1)}, bf16[128,512]{1,0:T(8,128)(2,1)S(1)}, u32[]{:S(2)}, u32[]{:S(2)}) collective-permute-start(bf16[128,512]{1,0:T(8,128)(2,1)S(1)} %slice.43.slot0), channel_id=1, source_target_pairs={{0,6},{2,4},{4,2},{6,0},{1,7},{3,5},{5,3},{7,1},{8,14},{10,12},{12... | collective-permute-start | bytes 393224 | tf_op jit(solution)/shard_map/ppermute | solution.py:36
  47.6 1.9 %collective-permute-start.2 = (bf16[128,512]{1,0:T(8,128)(2,1)S(1)}, bf16[128,512]{1,0:T(8,128)(2,1)S(1)}, u32[]{:S(2)}, u32[]{:S(2)}) collective-permute-start(bf16[128,512]{1,0:T(8,128)(2,1)S(1)} %slice.43.slot0), channel_id=1, source_target_pairs={{0,4},{2,6},{4,0},{6,2},{1,5},{3,7},{5,1},{7,3},{8,12},{10,14},{12... | collective-permute-start | bytes 393224 | tf_op jit(solution)/shard_map/ppermute | solution.py:36
  49.5 5.6 %collective-permute-start.1 = (bf16[128,512]{1,0:T(8,128)(2,1)S(1)}, bf16[128,512]{1,0:T(8,128)(2,1)S(1)}, u32[]{:S(2)}, u32[]{:S(2)}) collective-permute-start(bf16[128,512]{1,0:T(8,128)(2,1)S(1)} %slice.43.slot0), channel_id=1, source_target_pairs={{0,2},{2,0},{4,6},{6,4},{1,3},{3,1},{5,7},{7,5},{8,10},{10,8},{12,... | collective-permute-start | bytes 393224 | tf_op jit(solution)/shard_map/ppermute | solution.py:36
  55.1 0.1 pad_add_fusion.place_ref
  55.2 0.0 collective-permute-done.3.slot3
  55.2 4.4 %collective-permute-done.2.slot2 = bf16[128,512]{1,0:T(8,128)(2,1)S(1)} collective-permute-done((bf16[128,512]{1,0:T(8,128)(2,1)S(1)}, bf16[128,512]{1,0:T(8,128)(2,1)S(1)}, u32[]{:S(2)}, u32[]{:S(2)}) %collective-permute-start.2) | collective-permute-done | bytes 131104 | tf_op jit(solution)/shard_map/ppermute | solution.py:36
  59.6 1.1 collective-permute-done.1.slot1
  60.7 0.6 all-to-all-done.kv_ref
  61.2 0.0 copy-done.3
  61.2 1.2 shard_map.112
  62.4 8.0 %all_to_all.25.stats_ref = f32[4,4,512]{2,1,0:T(4,128)S(1)} all-to-all(f32[4,4,512]{2,1,0:T(4,128)S(1)} %broadcast_in_dim.5), channel_id=1, replica_groups=mesh['y'=4,'x'=4,'zh'=4,'zl'=4,'c'=2] {'zl'}, dimensions={0} | all-to-all | bytes 65536 | tf_op jit(solution)/shard_map/all_to_all | solution.py:48
  70.4 3.0 %shard_map.113 = (bf16[4,256,128]{2,1,0:T(8,128)(2,1)S(1)}, bf16[16,128,256]{2,1,0:T(8,128)(2,1)}) custom-call(s32[4]{0:T(128)S(1)} %pad_add_fusion.place_ref, s32[17]{0:T(128)S(1)} %copy-done.3, f32[4,4,512]{2,1,0:T(4,128)S(1)} %all_to_all.25.stats_ref, bf16[16,128,256]{2,1,0:T(8,128)(2,1)S(1)} %all-to-all-done.kv_ref, bf16[128,512]{1,0:T(8,128)(2,1)S(1)} %slice.43.slot0, ...), custom_call_target="tpu_custom_call" | custom-call | flops 1200000000 | bytes 4000000 | tf_op jit(solution)/shard_map/pallas_call | solution.py:183
  73.4 11.1 %all-to-all-start.2 = ((bf16[16,128,256]{2,1,0:T(8,128)(2,1)}), bf16[16,128,256]{2,1,0:T(8,128)(2,1)S(1)}, u32[]{:S(2)}, u32[]{:S(2)}) async-start(bf16[16,128,256]{2,1,0:T(8,128)(2,1)} %get-tuple-element.9), calls=%async_computation.2 | async-start | bytes 2097152 | tf_op jit(solution)/shard_map/all_to_all | solution.py:48
  84.5 2.7 %collective-permute-start.4 = (bf16[256,128]{1,0:T(8,128)(2,1)S(1)}, bf16[256,128]{1,0:T(8,128)(2,1)S(1)}, u32[]{:S(2)}, u32[]{:S(2)}) collective-permute-start(bf16[256,128]{1,0:T(8,128)(2,1)S(1)} %get-tuple-element.14), channel_id=1, source_target_pairs={{0,2},{2,0},{4,6},{6,4},{1,3},{3,1},{5,7},{7,5},{8,10},{10,8},{12,... | collective-permute-start | bytes 196616 | tf_op jit(solution)/shard_map/ppermute | solution.py:36
  87.2 3.3 %collective-permute-start.6 = (bf16[256,128]{1,0:T(8,128)(2,1)S(1)}, bf16[256,128]{1,0:T(8,128)(2,1)S(1)}, u32[]{:S(2)}, u32[]{:S(2)}) collective-permute-start(bf16[256,128]{1,0:T(8,128)(2,1)S(1)} %get-tuple-element.15), channel_id=1, source_target_pairs={{0,6},{2,4},{4,2},{6,0},{1,7},{3,5},{5,3},{7,1},{8,14},{10,12},{12... | collective-permute-start | bytes 196616 | tf_op jit(solution)/shard_map/ppermute | solution.py:36
  90.5 3.3 %collective-permute-start.5 = (bf16[256,128]{1,0:T(8,128)(2,1)S(1)}, bf16[256,128]{1,0:T(8,128)(2,1)S(1)}, u32[]{:S(2)}, u32[]{:S(2)}) collective-permute-start(bf16[256,128]{1,0:T(8,128)(2,1)S(1)} %get-tuple-element.16), channel_id=1, source_target_pairs={{0,4},{2,6},{4,0},{6,2},{1,5},{3,7},{5,1},{7,3},{8,12},{10,14},{12... | collective-permute-start | bytes 196616 | tf_op jit(solution)/shard_map/ppermute | solution.py:36
  93.8 4.6 %all-to-all-done.2 = bf16[16,128,256]{2,1,0:T(8,128)(2,1)S(1)} async-done(((bf16[16,128,256]{2,1,0:T(8,128)(2,1)}), bf16[16,128,256]{2,1,0:T(8,128)(2,1)S(1)}, u32[]{:S(2)}, u32[]{:S(2)}) %all-to-all-start.2) | async-done | bytes 1048608 | tf_op jit(solution)/shard_map/all_to_all | solution.py:48
  98.4 0.1 reduce_sum.33
  98.5 0.7 collective-permute-start.8
  99.2 0.0 collective-permute-done.4
  99.2 0.0 collective-permute-done.6
  99.2 0.0 collective-permute-done.5
  99.3 0.7 collective-permute-start.7
  100.0 0.0 collective-permute-done.8.kv_ref
  100.0 1.4 convolution_convert_fusion
  101.4 0.0 copy-start
  101.4 0.0 copy-start.1
  101.4 0.0 copy-start.2
  101.4 5.9 %all-to-all-start.3 = ((bf16[16,144,256]{2,1,0:T(8,128)(2,1)}), bf16[16,144,256]{2,1,0:T(8,128)(2,1)}, u32[]{:S(2)}, u32[]{:S(2)}) async-start(bf16[16,144,256]{2,1,0:T(8,128)(2,1)} %bitcast.37), calls=%async_computation.3 | async-start | bytes 2359296 | tf_op jit(solution)/shard_map/all_to_all | solution.py:48
  107.3 0.0 collective-permute-done.7.query_ref
  107.3 0.0 copy-done
  107.3 0.0 copy-done.1
  107.3 0.0 copy-done.2
  107.4 1.3 shard_map.114
  108.7 1.9 %collective-permute-start.9 = (bf16[4,288,128]{2,1,0:T(8,128)(2,1)S(1)}, bf16[4,288,128]{2,1,0:T(8,128)(2,1)S(1)}, u32[]{:S(2)}, u32[]{:S(2)}) collective-permute-start(bf16[4,288,128]{2,1,0:T(8,128)(2,1)S(1)} %slice_bitcast_fusion), channel_id=1, source_target_pairs={{0,1},{1,0},{2,3},{3,2},{4,5},{5,4},{6,7},{7,6},{8,9},{9,8},{10,11... | collective-permute-start | bytes 884744 | tf_op jit(solution)/shard_map/ppermute | solution.py:36
  110.6 1.5 collective-permute-done.9
  112.2 0.1 fusion
  112.3 10.3 %collective-permute-start.10 = (bf16[288,128]{1,0:T(8,128)(2,1)S(1)}, bf16[288,128]{1,0:T(8,128)(2,1)S(1)}, u32[]{:S(2)}, u32[]{:S(2)}) collective-permute-start(bf16[288,128]{1,0:T(8,128)(2,1)S(1)} %get-tuple-element.11), channel_id=1, source_target_pairs={{0,2},{2,0},{4,6},{6,4},{1,3},{3,1},{5,7},{7,5},{8,10},{10,8},{12,... | collective-permute-start | bytes 221192 | tf_op jit(solution)/shard_map/ppermute | solution.py:36
  122.6 9.6 %collective-permute-start.12 = (bf16[288,128]{1,0:T(8,128)(2,1)S(1)}, bf16[288,128]{1,0:T(8,128)(2,1)S(1)}, u32[]{:S(2)}, u32[]{:S(2)}) collective-permute-start(bf16[288,128]{1,0:T(8,128)(2,1)S(1)} %get-tuple-element.12), channel_id=1, source_target_pairs={{0,6},{2,4},{4,2},{6,0},{1,7},{3,5},{5,3},{7,1},{8,14},{10,12},{12... | collective-permute-start | bytes 221192 | tf_op jit(solution)/shard_map/ppermute | solution.py:36
  132.2 2.4 %collective-permute-start.11 = (bf16[288,128]{1,0:T(8,128)(2,1)S(1)}, bf16[288,128]{1,0:T(8,128)(2,1)S(1)}, u32[]{:S(2)}, u32[]{:S(2)}) collective-permute-start(bf16[288,128]{1,0:T(8,128)(2,1)S(1)} %get-tuple-element.13), channel_id=1, source_target_pairs={{0,4},{2,6},{4,0},{6,2},{1,5},{3,7},{5,1},{7,3},{8,12},{10,14},{12... | collective-permute-start | bytes 221192 | tf_op jit(solution)/shard_map/ppermute | solution.py:36
  134.6 0.0 all-to-all-done.3
  134.6 1.4 reduce_sum.34
  136.1 0.6 reshape.21
  136.7 8.2 %all-to-all-start.4 = ((bf16[4,36,256]{2,1,0:T(8,128)(2,1)}), bf16[4,36,256]{2,1,0:T(8,128)(2,1)S(1)}, u32[]{:S(2)}, u32[]{:S(2)}) async-start(bf16[4,36,256]{2,1,0:T(8,128)(2,1)} %reshape.21), calls=%async_computation.4 | async-start | bytes 163840 | tf_op jit(solution)/shard_map/all_to_all | solution.py:48
  144.9 0.0 collective-permute-done.10
  144.9 0.0 collective-permute-done.12
  144.9 0.0 collective-permute-done.11
  144.9 0.7 fusion.7
  145.6 12.2 %all-to-all-done.4 = bf16[4,36,256]{2,1,0:T(8,128)(2,1)S(1)} async-done(((bf16[4,36,256]{2,1,0:T(8,128)(2,1)}), bf16[4,36,256]{2,1,0:T(8,128)(2,1)S(1)}, u32[]{:S(2)}, u32[]{:S(2)}) %all-to-all-start.4) | async-done | bytes 73760 | tf_op jit(solution)/shard_map/all_to_all | solution.py:48
  157.9 0.6 fusion.8
  (8 shorter events, 0.1 us)
Async XLA Ops:
  1.5 34.7 %collective-permute-start = (bf16[128,768]{1,0:T(8,128)(2,1)S(1)}, bf16[128,768]{1,0:T(8,128)(2,1)S(1)}, u32[]{:S(2)}, u32[]{:S(2)}) collective-permute-start(bf16[128,768]{1,0:T(8,128)(2,1)S(1)} %pad_maximum_fusion), channel_id=1, source_target_pairs={{0,0},{2,8},{4,16},{6,24},{8,2},{10,10},{12,18},{14,26},{16,4},{18... | collective-permute-start | bytes 589832 | tf_op jit(solution)/shard_map/ppermute | solution.py:32
  37.3 23.9 %copy-start.3 = (s32[17]{0:T(128)S(1)}, s32[17]{0:T(128)}, u32[]{:S(2)}) copy-start(s32[17]{0:T(128)} %lengths_ref.3) | copy-start | bytes 208
  37.3 23.9 %all-to-all-start = ((bf16[16,128,256]{2,1,0:T(8,128)(2,1)}), bf16[16,128,256]{2,1,0:T(8,128)(2,1)S(1)}, u32[]{:S(2)}, u32[]{:S(2)}) async-start(bf16[16,128,256]{2,1,0:T(8,128)(2,1)} %broadcast_in_dim.4), calls=%async_computation | async-start | bytes 2097152 | tf_op jit(solution)/shard_map/all_to_all | solution.py:48
  44.9 10.2 %collective-permute-start.3 = (bf16[128,512]{1,0:T(8,128)(2,1)S(1)}, bf16[128,512]{1,0:T(8,128)(2,1)S(1)}, u32[]{:S(2)}, u32[]{:S(2)}) collective-permute-start(bf16[128,512]{1,0:T(8,128)(2,1)S(1)} %slice.43.slot0), channel_id=1, source_target_pairs={{0,6},{2,4},{4,2},{6,0},{1,7},{3,5},{5,3},{7,1},{8,14},{10,12},{12... | collective-permute-start | bytes 393224 | tf_op jit(solution)/shard_map/ppermute | solution.py:36
  47.6 12.0 %collective-permute-start.2 = (bf16[128,512]{1,0:T(8,128)(2,1)S(1)}, bf16[128,512]{1,0:T(8,128)(2,1)S(1)}, u32[]{:S(2)}, u32[]{:S(2)}) collective-permute-start(bf16[128,512]{1,0:T(8,128)(2,1)S(1)} %slice.43.slot0), channel_id=1, source_target_pairs={{0,4},{2,6},{4,0},{6,2},{1,5},{3,7},{5,1},{7,3},{8,12},{10,14},{12... | collective-permute-start | bytes 393224 | tf_op jit(solution)/shard_map/ppermute | solution.py:36
  49.5 11.1 %collective-permute-start.1 = (bf16[128,512]{1,0:T(8,128)(2,1)S(1)}, bf16[128,512]{1,0:T(8,128)(2,1)S(1)}, u32[]{:S(2)}, u32[]{:S(2)}) collective-permute-start(bf16[128,512]{1,0:T(8,128)(2,1)S(1)} %slice.43.slot0), channel_id=1, source_target_pairs={{0,2},{2,0},{4,6},{6,4},{1,3},{3,1},{5,7},{7,5},{8,10},{10,8},{12,... | collective-permute-start | bytes 393224 | tf_op jit(solution)/shard_map/ppermute | solution.py:36
  73.4 25.0 %all-to-all-start.2 = ((bf16[16,128,256]{2,1,0:T(8,128)(2,1)}), bf16[16,128,256]{2,1,0:T(8,128)(2,1)S(1)}, u32[]{:S(2)}, u32[]{:S(2)}) async-start(bf16[16,128,256]{2,1,0:T(8,128)(2,1)} %get-tuple-element.9), calls=%async_computation.2 | async-start | bytes 2097152 | tf_op jit(solution)/shard_map/all_to_all | solution.py:48
  84.5 14.7 %collective-permute-start.4 = (bf16[256,128]{1,0:T(8,128)(2,1)S(1)}, bf16[256,128]{1,0:T(8,128)(2,1)S(1)}, u32[]{:S(2)}, u32[]{:S(2)}) collective-permute-start(bf16[256,128]{1,0:T(8,128)(2,1)S(1)} %get-tuple-element.14), channel_id=1, source_target_pairs={{0,2},{2,0},{4,6},{6,4},{1,3},{3,1},{5,7},{7,5},{8,10},{10,8},{12,... | collective-permute-start | bytes 196616 | tf_op jit(solution)/shard_map/ppermute | solution.py:36
  87.2 12.0 %collective-permute-start.6 = (bf16[256,128]{1,0:T(8,128)(2,1)S(1)}, bf16[256,128]{1,0:T(8,128)(2,1)S(1)}, u32[]{:S(2)}, u32[]{:S(2)}) collective-permute-start(bf16[256,128]{1,0:T(8,128)(2,1)S(1)} %get-tuple-element.15), channel_id=1, source_target_pairs={{0,6},{2,4},{4,2},{6,0},{1,7},{3,5},{5,3},{7,1},{8,14},{10,12},{12... | collective-permute-start | bytes 196616 | tf_op jit(solution)/shard_map/ppermute | solution.py:36
  90.5 8.8 %collective-permute-start.5 = (bf16[256,128]{1,0:T(8,128)(2,1)S(1)}, bf16[256,128]{1,0:T(8,128)(2,1)S(1)}, u32[]{:S(2)}, u32[]{:S(2)}) collective-permute-start(bf16[256,128]{1,0:T(8,128)(2,1)S(1)} %get-tuple-element.16), channel_id=1, source_target_pairs={{0,4},{2,6},{4,0},{6,2},{1,5},{3,7},{5,1},{7,3},{8,12},{10,14},{12... | collective-permute-start | bytes 196616 | tf_op jit(solution)/shard_map/ppermute | solution.py:36
  98.5 1.4 collective-permute-start.8
  99.3 8.0 %collective-permute-start.7 = (bf16[256,128]{1,0:T(8,128)(2,1)S(1)}, bf16[256,128]{1,0:T(8,128)(2,1)S(1)}, u32[]{:S(2)}, u32[]{:S(2)}) collective-permute-start(bf16[256,128]{1,0:T(8,128)(2,1)S(1)} %fusion.6), channel_id=1, source_target_pairs={{0,0},{2,8},{4,16},{6,24},{8,2},{10,10},{12,18},{14,26},{16,4},{18... | collective-permute-start | bytes 196616 | tf_op jit(solution)/shard_map/ppermute | solution.py:32
  101.4 5.9 %copy-start = (bf16[2304,256]{1,0:T(8,128)(2,1)S(1)}, bf16[2304,256]{1,0:T(8,128)(2,1)}, u32[]{:S(2)}) copy-start(bf16[2304,256]{1,0:T(8,128)(2,1)} %wq_ref.1) | copy-start | bytes 3538948
  101.4 5.9 %copy-start.1 = (bf16[2304,128]{1,0:T(8,128)(2,1)S(1)}, bf16[2304,128]{1,0:T(8,128)(2,1)}, u32[]{:S(2)}) copy-start(bf16[2304,128]{1,0:T(8,128)(2,1)} %wk_ref.1) | copy-start | bytes 1769476
  101.4 5.9 %copy-start.2 = (bf16[2304,128]{1,0:T(8,128)(2,1)S(1)}, bf16[2304,128]{1,0:T(8,128)(2,1)}, u32[]{:S(2)}) copy-start(bf16[2304,128]{1,0:T(8,128)(2,1)} %wv_ref.1) | copy-start | bytes 1769476
  101.4 33.2 %all-to-all-start.3 = ((bf16[16,144,256]{2,1,0:T(8,128)(2,1)}), bf16[16,144,256]{2,1,0:T(8,128)(2,1)}, u32[]{:S(2)}, u32[]{:S(2)}) async-start(bf16[16,144,256]{2,1,0:T(8,128)(2,1)} %bitcast.37), calls=%async_computation.3 | async-start | bytes 2359296 | tf_op jit(solution)/shard_map/all_to_all | solution.py:48
  108.7 3.5 %collective-permute-start.9 = (bf16[4,288,128]{2,1,0:T(8,128)(2,1)S(1)}, bf16[4,288,128]{2,1,0:T(8,128)(2,1)S(1)}, u32[]{:S(2)}, u32[]{:S(2)}) collective-permute-start(bf16[4,288,128]{2,1,0:T(8,128)(2,1)S(1)} %slice_bitcast_fusion), channel_id=1, source_target_pairs={{0,1},{1,0},{2,3},{3,2},{4,5},{5,4},{6,7},{7,6},{8,9},{9,8},{10,11... | collective-permute-start | bytes 884744 | tf_op jit(solution)/shard_map/ppermute | solution.py:36
  112.3 32.6 %collective-permute-start.10 = (bf16[288,128]{1,0:T(8,128)(2,1)S(1)}, bf16[288,128]{1,0:T(8,128)(2,1)S(1)}, u32[]{:S(2)}, u32[]{:S(2)}) collective-permute-start(bf16[288,128]{1,0:T(8,128)(2,1)S(1)} %get-tuple-element.11), channel_id=1, source_target_pairs={{0,2},{2,0},{4,6},{6,4},{1,3},{3,1},{5,7},{7,5},{8,10},{10,8},{12,... | collective-permute-start | bytes 221192 | tf_op jit(solution)/shard_map/ppermute | solution.py:36
  122.6 22.3 %collective-permute-start.12 = (bf16[288,128]{1,0:T(8,128)(2,1)S(1)}, bf16[288,128]{1,0:T(8,128)(2,1)S(1)}, u32[]{:S(2)}, u32[]{:S(2)}) collective-permute-start(bf16[288,128]{1,0:T(8,128)(2,1)S(1)} %get-tuple-element.12), channel_id=1, source_target_pairs={{0,6},{2,4},{4,2},{6,0},{1,7},{3,5},{5,3},{7,1},{8,14},{10,12},{12... | collective-permute-start | bytes 221192 | tf_op jit(solution)/shard_map/ppermute | solution.py:36
  132.2 12.7 %collective-permute-start.11 = (bf16[288,128]{1,0:T(8,128)(2,1)S(1)}, bf16[288,128]{1,0:T(8,128)(2,1)S(1)}, u32[]{:S(2)}, u32[]{:S(2)}) collective-permute-start(bf16[288,128]{1,0:T(8,128)(2,1)S(1)} %get-tuple-element.13), channel_id=1, source_target_pairs={{0,4},{2,6},{4,0},{6,2},{1,5},{3,7},{5,1},{7,3},{8,12},{10,14},{12... | collective-permute-start | bytes 221192 | tf_op jit(solution)/shard_map/ppermute | solution.py:36
  136.7 21.1 %all-to-all-start.4 = ((bf16[4,36,256]{2,1,0:T(8,128)(2,1)}), bf16[4,36,256]{2,1,0:T(8,128)(2,1)S(1)}, u32[]{:S(2)}, u32[]{:S(2)}) async-start(bf16[4,36,256]{2,1,0:T(8,128)(2,1)} %reshape.21), calls=%async_computation.4 | async-start | bytes 163840 | tf_op jit(solution)/shard_map/all_to_all | solution.py:48

commit v4 on v3

--- a/solution.py
+++ b/solution.py
@@ -216,12 +216,14 @@
     )
     kv_parts = exchange(kv_parts, PLANE)
     query_parts = returned([query_parts[slot] for slot in range(GROUP)], "zl")
-    grad_query = swapped(sum(part.astype(F32) for part in query_parts).astype(BF16))
+    grad_query = sum(part.astype(F32) for part in query_parts).astype(BF16)
     grad_kv = added(kv_parts).astype(BF16)
 
     grad_kv = swapped(grad_kv)
 
     weight = dot(features, grad_kv, NN).astype(BF16).reshape(BLOCKS, -1, 2 * WIDTH)
+    _, grad_query = lax.optimization_barrier((weight, grad_query))
+    grad_query = swapped(grad_query)
     weight = added(exchange(weight, PLANE)).astype(BF16).reshape(GROUP, -1, 2 * WIDTH)
     weight = added(exchange(weight, "zh"))
 

time: 160 us -> 167 us (1.044)
  starting transfers between devices: 78.4 us -> 85.9 us
    ppermute x10, starting transfers between devices: 43.5 us -> 51 us  [partner(): lax.ppermute(value, axis, [(i, i ^ mask) for i in range(lax.axis_size(axi...]
  transfers between devices with their start and end apart: 17 -> 17, of which waited for: 6 -> 6; matrix products, arithmetic and copies ran while one was open for 3% -> 2% of each run, Pallas kernels for 1% -> 1%
where the time goes in v4:
time: 167 us; the launch traced here: 166 us
  starting transfers between devices  85.9 us (51%)
  blocking collectives  42 us (25%)
  waiting for transfers between devices  24.7 us (15%)
  Pallas kernels  5.48 us (3%)
  other arithmetic  3.37 us (2%)
  local copies, waits for them, and re-layouts  2.44 us (1%)
    ppermute x10, starting transfers between devices, partner(): lax.ppermute(value, axis, [(i, i ^ mask) for i in range(lax.axis_size(axi...  51 us
    all_gather x1, blocking collectives, shards(): features = lax.all_gather(inputs.T, ('zl', 'c'), axis=0, tiled=True)  34 us
    all_to_all x4, starting transfers between devices, exchange(): return lax.all_to_all(parts, axes, 0, 0, tiled=True)  32.8 us
    all_to_all x4, waiting for transfers between devices, exchange(): return lax.all_to_all(parts, axes, 0, 0, tiled=True)  17.6 us
    all_to_all x1, blocking collectives, exchange(): return lax.all_to_all(parts, axes, 0, 0, tiled=True)  8.01 us
    ppermute x10, waiting for transfers between devices, partner(): lax.ppermute(value, axis, [(i, i ^ mask) for i in range(lax.axis_size(axi...  7.06 us
    pallas_call x3, Pallas kernels, run_kernel(): pl.pallas_call(body, out_shape=shapes, in_specs=[smem] * len(scalars) + [...  5.48 us
  transfers between devices with their start and end apart: 17, of which 6 were waited for; matrix products, arithmetic and copies ran while one was open for 2% of the time, Pallas kernels for 1%

profile of v4, /device:TPU:2, one launch (start us, length us, event | category | flops | bytes accessed | tf_op | source)
XLA Modules:
  0.0 166.2 jit_solution(4989983172615113651)
XLA Ops:
  0.6 0.9 pad_maximum_fusion
  1.5 0.7 collective-permute-start
  2.2 34.0 %all_gather.3 = bf16[2304,128]{1,0:T(8,128)(2,1)S(1)} all-gather(bf16[288,128]{1,0:T(8,128)(2,1)} %bitcast.38), channel_id=1, replica_groups=mesh['y'=4,'x'=4,'zh'=4,'zl'=4,'c'=2] {'zl','c'}, dimensions={0}, use_global_device_ids=true | all-gather | bytes 663552 | tf_op jit(solution)/shard_map/all_gather | solution.py:200
  36.2 0.0 collective-permute-done
  36.2 1.1 broadcast_in_dim.4
  37.3 0.0 copy-start.3
  37.3 7.6 %all-to-all-start = ((bf16[16,128,256]{2,1,0:T(8,128)(2,1)}), bf16[16,128,256]{2,1,0:T(8,128)(2,1)S(1)}, u32[]{:S(2)}, u32[]{:S(2)}) async-start(bf16[16,128,256]{2,1,0:T(8,128)(2,1)} %broadcast_in_dim.4), calls=%async_computation | async-start | bytes 2097152 | tf_op jit(solution)/shard_map/all_to_all | solution.py:48
  44.9 2.6 %collective-permute-start.3 = (bf16[128,512]{1,0:T(8,128)(2,1)S(1)}, bf16[128,512]{1,0:T(8,128)(2,1)S(1)}, u32[]{:S(2)}, u32[]{:S(2)}) collective-permute-start(bf16[128,512]{1,0:T(8,128)(2,1)S(1)} %slice.43.slot0), channel_id=1, source_target_pairs={{0,6},{2,4},{4,2},{6,0},{1,7},{3,5},{5,3},{7,1},{8,14},{10,12},{12... | collective-permute-start | bytes 393224 | tf_op jit(solution)/shard_map/ppermute | solution.py:36
  47.6 1.9 %collective-permute-start.2 = (bf16[128,512]{1,0:T(8,128)(2,1)S(1)}, bf16[128,512]{1,0:T(8,128)(2,1)S(1)}, u32[]{:S(2)}, u32[]{:S(2)}) collective-permute-start(bf16[128,512]{1,0:T(8,128)(2,1)S(1)} %slice.43.slot0), channel_id=1, source_target_pairs={{0,4},{2,6},{4,0},{6,2},{1,5},{3,7},{5,1},{7,3},{8,12},{10,14},{12... | collective-permute-start | bytes 393224 | tf_op jit(solution)/shard_map/ppermute | solution.py:36
  49.5 5.6 %collective-permute-start.1 = (bf16[128,512]{1,0:T(8,128)(2,1)S(1)}, bf16[128,512]{1,0:T(8,128)(2,1)S(1)}, u32[]{:S(2)}, u32[]{:S(2)}) collective-permute-start(bf16[128,512]{1,0:T(8,128)(2,1)S(1)} %slice.43.slot0), channel_id=1, source_target_pairs={{0,2},{2,0},{4,6},{6,4},{1,3},{3,1},{5,7},{7,5},{8,10},{10,8},{12,... | collective-permute-start | bytes 393224 | tf_op jit(solution)/shard_map/ppermute | solution.py:36
  55.1 0.1 pad_add_fusion.place_ref
  55.2 0.0 collective-permute-done.3.slot3
  55.2 4.4 %collective-permute-done.2.slot2 = bf16[128,512]{1,0:T(8,128)(2,1)S(1)} collective-permute-done((bf16[128,512]{1,0:T(8,128)(2,1)S(1)}, bf16[128,512]{1,0:T(8,128)(2,1)S(1)}, u32[]{:S(2)}, u32[]{:S(2)}) %collective-permute-start.2) | collective-permute-done | bytes 131104 | tf_op jit(solution)/shard_map/ppermute | solution.py:36
  59.6 1.1 collective-permute-done.1.slot1
  60.7 0.6 all-to-all-done.kv_ref
  61.2 0.0 copy-done.3
  61.2 1.2 shard_map.112
  62.4 8.0 %all_to_all.25.stats_ref = f32[4,4,512]{2,1,0:T(4,128)S(1)} all-to-all(f32[4,4,512]{2,1,0:T(4,128)S(1)} %broadcast_in_dim.5), channel_id=1, replica_groups=mesh['y'=4,'x'=4,'zh'=4,'zl'=4,'c'=2] {'zl'}, dimensions={0} | all-to-all | bytes 65536 | tf_op jit(solution)/shard_map/all_to_all | solution.py:48
  70.4 3.0 %shard_map.113 = (bf16[4,256,128]{2,1,0:T(8,128)(2,1)S(1)}, bf16[16,128,256]{2,1,0:T(8,128)(2,1)}) custom-call(s32[4]{0:T(128)S(1)} %pad_add_fusion.place_ref, s32[17]{0:T(128)S(1)} %copy-done.3, f32[4,4,512]{2,1,0:T(4,128)S(1)} %all_to_all.25.stats_ref, bf16[16,128,256]{2,1,0:T(8,128)(2,1)S(1)} %all-to-all-done.kv_ref, bf16[128,512]{1,0:T(8,128)(2,1)S(1)} %slice.43.slot0, ...), custom_call_target="tpu_custom_call" | custom-call | flops 1200000000 | bytes 4000000 | tf_op jit(solution)/shard_map/pallas_call | solution.py:183
  73.4 10.7 %all-to-all-start.2 = ((bf16[16,128,256]{2,1,0:T(8,128)(2,1)}), bf16[16,128,256]{2,1,0:T(8,128)(2,1)S(1)}, u32[]{:S(2)}, u32[]{:S(2)}) async-start(bf16[16,128,256]{2,1,0:T(8,128)(2,1)} %get-tuple-element.10), calls=%async_computation.2 | async-start | bytes 2097152 | tf_op jit(solution)/shard_map/all_to_all | solution.py:48
  84.2 2.7 %collective-permute-start.5 = (bf16[256,128]{1,0:T(8,128)(2,1)S(1)}, bf16[256,128]{1,0:T(8,128)(2,1)S(1)}, u32[]{:S(2)}, u32[]{:S(2)}) collective-permute-start(bf16[256,128]{1,0:T(8,128)(2,1)S(1)} %get-tuple-element.16), channel_id=1, source_target_pairs={{0,2},{2,0},{4,6},{6,4},{1,3},{3,1},{5,7},{7,5},{8,10},{10,8},{12,... | collective-permute-start | bytes 196616 | tf_op jit(solution)/shard_map/ppermute | solution.py:36
  86.8 3.3 %collective-permute-start.7 = (bf16[256,128]{1,0:T(8,128)(2,1)S(1)}, bf16[256,128]{1,0:T(8,128)(2,1)S(1)}, u32[]{:S(2)}, u32[]{:S(2)}) collective-permute-start(bf16[256,128]{1,0:T(8,128)(2,1)S(1)} %get-tuple-element.17), channel_id=1, source_target_pairs={{0,6},{2,4},{4,2},{6,0},{1,7},{3,5},{5,3},{7,1},{8,14},{10,12},{12... | collective-permute-start | bytes 196616 | tf_op jit(solution)/shard_map/ppermute | solution.py:36
  90.1 3.3 %collective-permute-start.6 = (bf16[256,128]{1,0:T(8,128)(2,1)S(1)}, bf16[256,128]{1,0:T(8,128)(2,1)S(1)}, u32[]{:S(2)}, u32[]{:S(2)}) collective-permute-start(bf16[256,128]{1,0:T(8,128)(2,1)S(1)} %get-tuple-element.18), channel_id=1, source_target_pairs={{0,4},{2,6},{4,0},{6,2},{1,5},{3,7},{5,1},{7,3},{8,12},{10,14},{12... | collective-permute-start | bytes 196616 | tf_op jit(solution)/shard_map/ppermute | solution.py:36
  93.4 4.6 %all-to-all-done.2 = bf16[16,128,256]{2,1,0:T(8,128)(2,1)S(1)} async-done(((bf16[16,128,256]{2,1,0:T(8,128)(2,1)}), bf16[16,128,256]{2,1,0:T(8,128)(2,1)S(1)}, u32[]{:S(2)}, u32[]{:S(2)}) %all-to-all-start.2) | async-done | bytes 1048608 | tf_op jit(solution)/shard_map/all_to_all | solution.py:48
  98.0 0.1 reduce_sum.33
  98.1 0.7 collective-permute-start.4
  98.8 0.0 collective-permute-done.5
  98.8 0.0 collective-permute-done.7
  98.8 0.0 collective-permute-done.6
  98.9 0.0 collective-permute-done.4.kv_ref
  98.9 1.4 convolution_convert_fusion
  100.3 0.0 copy-start
  100.3 0.0 copy-start.1
  100.3 0.0 copy-start.2
  100.3 0.8 collective-permute-start.8
  101.1 5.8 %all-to-all-start.3 = ((bf16[16,144,256]{2,1,0:T(8,128)(2,1)}), bf16[16,144,256]{2,1,0:T(8,128)(2,1)}, u32[]{:S(2)}, u32[]{:S(2)}) async-start(bf16[16,144,256]{2,1,0:T(8,128)(2,1)} %bitcast.37), calls=%async_computation.3 | async-start | bytes 2359296 | tf_op jit(solution)/shard_map/all_to_all | solution.py:48
  107.0 0.0 collective-permute-done.8.query_ref
  107.0 0.0 copy-done
  107.0 0.0 copy-done.1
  107.0 0.0 copy-done.2
  107.0 1.3 shard_map.114
  108.4 1.9 %collective-permute-start.9 = (bf16[4,288,128]{2,1,0:T(8,128)(2,1)S(1)}, bf16[4,288,128]{2,1,0:T(8,128)(2,1)S(1)}, u32[]{:S(2)}, u32[]{:S(2)}) collective-permute-start(bf16[4,288,128]{2,1,0:T(8,128)(2,1)S(1)} %slice_bitcast_fusion), channel_id=1, source_target_pairs={{0,1},{1,0},{2,3},{3,2},{4,5},{5,4},{6,7},{7,6},{8,9},{9,8},{10,11... | collective-permute-start | bytes 884744 | tf_op jit(solution)/shard_map/ppermute | solution.py:36
  110.3 1.5 collective-permute-done.9
  111.8 0.1 fusion
  111.9 13.7 %collective-permute-start.10 = (bf16[288,128]{1,0:T(8,128)(2,1)S(1)}, bf16[288,128]{1,0:T(8,128)(2,1)S(1)}, u32[]{:S(2)}, u32[]{:S(2)}) collective-permute-start(bf16[288,128]{1,0:T(8,128)(2,1)S(1)} %get-tuple-element.13), channel_id=1, source_target_pairs={{0,2},{2,0},{4,6},{6,4},{1,3},{3,1},{5,7},{7,5},{8,10},{10,8},{12,... | collective-permute-start | bytes 221192 | tf_op jit(solution)/shard_map/ppermute | solution.py:36
  125.7 13.5 %collective-permute-start.12 = (bf16[288,128]{1,0:T(8,128)(2,1)S(1)}, bf16[288,128]{1,0:T(8,128)(2,1)S(1)}, u32[]{:S(2)}, u32[]{:S(2)}) collective-permute-start(bf16[288,128]{1,0:T(8,128)(2,1)S(1)} %get-tuple-element.14), channel_id=1, source_target_pairs={{0,6},{2,4},{4,2},{6,0},{1,7},{3,5},{5,3},{7,1},{8,14},{10,12},{12... | collective-permute-start | bytes 221192 | tf_op jit(solution)/shard_map/ppermute | solution.py:36
  139.2 2.5 %collective-permute-start.11 = (bf16[288,128]{1,0:T(8,128)(2,1)S(1)}, bf16[288,128]{1,0:T(8,128)(2,1)S(1)}, u32[]{:S(2)}, u32[]{:S(2)}) collective-permute-start(bf16[288,128]{1,0:T(8,128)(2,1)S(1)} %get-tuple-element.15), channel_id=1, source_target_pairs={{0,4},{2,6},{4,0},{6,2},{1,5},{3,7},{5,1},{7,3},{8,12},{10,14},{12... | collective-permute-start | bytes 221192 | tf_op jit(solution)/shard_map/ppermute | solution.py:36
  141.7 0.0 all-to-all-done.3
  141.7 1.4 reduce_sum.34
  143.1 0.6 reshape.21
  143.8 8.7 %all-to-all-start.4 = ((bf16[4,36,256]{2,1,0:T(8,128)(2,1)}), bf16[4,36,256]{2,1,0:T(8,128)(2,1)S(1)}, u32[]{:S(2)}, u32[]{:S(2)}) async-start(bf16[4,36,256]{2,1,0:T(8,128)(2,1)} %reshape.21), calls=%async_computation.4 | async-start | bytes 163840 | tf_op jit(solution)/shard_map/all_to_all | solution.py:48
  152.4 0.0 collective-permute-done.10
  152.4 0.0 collective-permute-done.12
  152.4 0.0 collective-permute-done.11
  152.5 0.7 fusion.7
  153.1 12.4 %all-to-all-done.4 = bf16[4,36,256]{2,1,0:T(8,128)(2,1)S(1)} async-done(((bf16[4,36,256]{2,1,0:T(8,128)(2,1)}), bf16[4,36,256]{2,1,0:T(8,128)(2,1)S(1)}, u32[]{:S(2)}, u32[]{:S(2)}) %all-to-all-start.4) | async-done | bytes 73760 | tf_op jit(solution)/shard_map/all_to_all | solution.py:48
  165.6 0.6 fusion.8
  (8 shorter events, 0.1 us)
Async XLA Ops:
  1.5 34.7 %collective-permute-start = (bf16[128,768]{1,0:T(8,128)(2,1)S(1)}, bf16[128,768]{1,0:T(8,128)(2,1)S(1)}, u32[]{:S(2)}, u32[]{:S(2)}) collective-permute-start(bf16[128,768]{1,0:T(8,128)(2,1)S(1)} %pad_maximum_fusion), channel_id=1, source_target_pairs={{0,0},{2,8},{4,16},{6,24},{8,2},{10,10},{12,18},{14,26},{16,4},{18... | collective-permute-start | bytes 589832 | tf_op jit(solution)/shard_map/ppermute | solution.py:32
  37.3 23.9 %copy-start.3 = (s32[17]{0:T(128)S(1)}, s32[17]{0:T(128)}, u32[]{:S(2)}) copy-start(s32[17]{0:T(128)} %lengths_ref.3) | copy-start | bytes 208
  37.3 23.9 %all-to-all-start = ((bf16[16,128,256]{2,1,0:T(8,128)(2,1)}), bf16[16,128,256]{2,1,0:T(8,128)(2,1)S(1)}, u32[]{:S(2)}, u32[]{:S(2)}) async-start(bf16[16,128,256]{2,1,0:T(8,128)(2,1)} %broadcast_in_dim.4), calls=%async_computation | async-start | bytes 2097152 | tf_op jit(solution)/shard_map/all_to_all | solution.py:48
  44.9 10.2 %collective-permute-start.3 = (bf16[128,512]{1,0:T(8,128)(2,1)S(1)}, bf16[128,512]{1,0:T(8,128)(2,1)S(1)}, u32[]{:S(2)}, u32[]{:S(2)}) collective-permute-start(bf16[128,512]{1,0:T(8,128)(2,1)S(1)} %slice.43.slot0), channel_id=1, source_target_pairs={{0,6},{2,4},{4,2},{6,0},{1,7},{3,5},{5,3},{7,1},{8,14},{10,12},{12... | collective-permute-start | bytes 393224 | tf_op jit(solution)/shard_map/ppermute | solution.py:36
  47.6 12.0 %collective-permute-start.2 = (bf16[128,512]{1,0:T(8,128)(2,1)S(1)}, bf16[128,512]{1,0:T(8,128)(2,1)S(1)}, u32[]{:S(2)}, u32[]{:S(2)}) collective-permute-start(bf16[128,512]{1,0:T(8,128)(2,1)S(1)} %slice.43.slot0), channel_id=1, source_target_pairs={{0,4},{2,6},{4,0},{6,2},{1,5},{3,7},{5,1},{7,3},{8,12},{10,14},{12... | collective-permute-start | bytes 393224 | tf_op jit(solution)/shard_map/ppermute | solution.py:36
  49.5 11.1 %collective-permute-start.1 = (bf16[128,512]{1,0:T(8,128)(2,1)S(1)}, bf16[128,512]{1,0:T(8,128)(2,1)S(1)}, u32[]{:S(2)}, u32[]{:S(2)}) collective-permute-start(bf16[128,512]{1,0:T(8,128)(2,1)S(1)} %slice.43.slot0), channel_id=1, source_target_pairs={{0,2},{2,0},{4,6},{6,4},{1,3},{3,1},{5,7},{7,5},{8,10},{10,8},{12,... | collective-permute-start | bytes 393224 | tf_op jit(solution)/shard_map/ppermute | solution.py:36
  73.4 24.6 %all-to-all-start.2 = ((bf16[16,128,256]{2,1,0:T(8,128)(2,1)}), bf16[16,128,256]{2,1,0:T(8,128)(2,1)S(1)}, u32[]{:S(2)}, u32[]{:S(2)}) async-start(bf16[16,128,256]{2,1,0:T(8,128)(2,1)} %get-tuple-element.10), calls=%async_computation.2 | async-start | bytes 2097152 | tf_op jit(solution)/shard_map/all_to_all | solution.py:48
  84.2 14.6 %collective-permute-start.5 = (bf16[256,128]{1,0:T(8,128)(2,1)S(1)}, bf16[256,128]{1,0:T(8,128)(2,1)S(1)}, u32[]{:S(2)}, u32[]{:S(2)}) collective-permute-start(bf16[256,128]{1,0:T(8,128)(2,1)S(1)} %get-tuple-element.16), channel_id=1, source_target_pairs={{0,2},{2,0},{4,6},{6,4},{1,3},{3,1},{5,7},{7,5},{8,10},{10,8},{12,... | collective-permute-start | bytes 196616 | tf_op jit(solution)/shard_map/ppermute | solution.py:36
  86.8 12.0 %collective-permute-start.7 = (bf16[256,128]{1,0:T(8,128)(2,1)S(1)}, bf16[256,128]{1,0:T(8,128)(2,1)S(1)}, u32[]{:S(2)}, u32[]{:S(2)}) collective-permute-start(bf16[256,128]{1,0:T(8,128)(2,1)S(1)} %get-tuple-element.17), channel_id=1, source_target_pairs={{0,6},{2,4},{4,2},{6,0},{1,7},{3,5},{5,3},{7,1},{8,14},{10,12},{12... | collective-permute-start | bytes 196616 | tf_op jit(solution)/shard_map/ppermute | solution.py:36
  90.1 8.7 %collective-permute-start.6 = (bf16[256,128]{1,0:T(8,128)(2,1)S(1)}, bf16[256,128]{1,0:T(8,128)(2,1)S(1)}, u32[]{:S(2)}, u32[]{:S(2)}) collective-permute-start(bf16[256,128]{1,0:T(8,128)(2,1)S(1)} %get-tuple-element.18), channel_id=1, source_target_pairs={{0,4},{2,6},{4,0},{6,2},{1,5},{3,7},{5,1},{7,3},{8,12},{10,14},{12... | collective-permute-start | bytes 196616 | tf_op jit(solution)/shard_map/ppermute | solution.py:36
  98.1 0.8 collective-permute-start.4
  100.3 6.6 %copy-start = (bf16[2304,256]{1,0:T(8,128)(2,1)S(1)}, bf16[2304,256]{1,0:T(8,128)(2,1)}, u32[]{:S(2)}) copy-start(bf16[2304,256]{1,0:T(8,128)(2,1)} %wq_ref.1) | copy-start | bytes 3538948
  100.3 6.6 %copy-start.1 = (bf16[2304,128]{1,0:T(8,128)(2,1)S(1)}, bf16[2304,128]{1,0:T(8,128)(2,1)}, u32[]{:S(2)}) copy-start(bf16[2304,128]{1,0:T(8,128)(2,1)} %wk_ref.1) | copy-start | bytes 1769476
  100.3 6.6 %copy-start.2 = (bf16[2304,128]{1,0:T(8,128)(2,1)S(1)}, bf16[2304,128]{1,0:T(8,128)(2,1)}, u32[]{:S(2)}) copy-start(bf16[2304,128]{1,0:T(8,128)(2,1)} %wv_ref.1) | copy-start | bytes 1769476
  100.3 6.6 %collective-permute-start.8 = (bf16[256,128]{1,0:T(8,128)(2,1)S(1)}, bf16[256,128]{1,0:T(8,128)(2,1)S(1)}, u32[]{:S(2)}, u32[]{:S(2)}) collective-permute-start(bf16[256,128]{1,0:T(8,128)(2,1)S(1)} %fusion.6), channel_id=1, source_target_pairs={{0,0},{2,8},{4,16},{6,24},{8,2},{10,10},{12,18},{14,26},{16,4},{18... | collective-permute-start | bytes 196616 | tf_op jit(solution)/shard_map/ppermute | solution.py:32
  101.1 40.5 %all-to-all-start.3 = ((bf16[16,144,256]{2,1,0:T(8,128)(2,1)}), bf16[16,144,256]{2,1,0:T(8,128)(2,1)}, u32[]{:S(2)}, u32[]{:S(2)}) async-start(bf16[16,144,256]{2,1,0:T(8,128)(2,1)} %bitcast.37), calls=%async_computation.3 | async-start | bytes 2359296 | tf_op jit(solution)/shard_map/all_to_all | solution.py:48
  108.4 3.5 %collective-permute-start.9 = (bf16[4,288,128]{2,1,0:T(8,128)(2,1)S(1)}, bf16[4,288,128]{2,1,0:T(8,128)(2,1)S(1)}, u32[]{:S(2)}, u32[]{:S(2)}) collective-permute-start(bf16[4,288,128]{2,1,0:T(8,128)(2,1)S(1)} %slice_bitcast_fusion), channel_id=1, source_target_pairs={{0,1},{1,0},{2,3},{3,2},{4,5},{5,4},{6,7},{7,6},{8,9},{9,8},{10,11... | collective-permute-start | bytes 884744 | tf_op jit(solution)/shard_map/ppermute | solution.py:36
  111.9 40.5 %collective-permute-start.10 = (bf16[288,128]{1,0:T(8,128)(2,1)S(1)}, bf16[288,128]{1,0:T(8,128)(2,1)S(1)}, u32[]{:S(2)}, u32[]{:S(2)}) collective-permute-start(bf16[288,128]{1,0:T(8,128)(2,1)S(1)} %get-tuple-element.13), channel_id=1, source_target_pairs={{0,2},{2,0},{4,6},{6,4},{1,3},{3,1},{5,7},{7,5},{8,10},{10,8},{12,... | collective-permute-start | bytes 221192 | tf_op jit(solution)/shard_map/ppermute | solution.py:36
  125.7 26.7 %collective-permute-start.12 = (bf16[288,128]{1,0:T(8,128)(2,1)S(1)}, bf16[288,128]{1,0:T(8,128)(2,1)S(1)}, u32[]{:S(2)}, u32[]{:S(2)}) collective-permute-start(bf16[288,128]{1,0:T(8,128)(2,1)S(1)} %get-tuple-element.14), channel_id=1, source_target_pairs={{0,6},{2,4},{4,2},{6,0},{1,7},{3,5},{5,3},{7,1},{8,14},{10,12},{12... | collective-permute-start | bytes 221192 | tf_op jit(solution)/shard_map/ppermute | solution.py:36
  139.2 13.3 %collective-permute-start.11 = (bf16[288,128]{1,0:T(8,128)(2,1)S(1)}, bf16[288,128]{1,0:T(8,128)(2,1)S(1)}, u32[]{:S(2)}, u32[]{:S(2)}) collective-permute-start(bf16[288,128]{1,0:T(8,128)(2,1)S(1)} %get-tuple-element.15), channel_id=1, source_target_pairs={{0,4},{2,6},{4,0},{6,2},{1,5},{3,7},{5,1},{7,3},{8,12},{10,14},{12... | collective-permute-start | bytes 221192 | tf_op jit(solution)/shard_map/ppermute | solution.py:36
  143.8 21.8 %all-to-all-start.4 = ((bf16[4,36,256]{2,1,0:T(8,128)(2,1)}), bf16[4,36,256]{2,1,0:T(8,128)(2,1)S(1)}, u32[]{:S(2)}, u32[]{:S(2)}) async-start(bf16[4,36,256]{2,1,0:T(8,128)(2,1)} %reshape.21), calls=%async_computation.4 | async-start | bytes 163840 | tf_op jit(solution)/shard_map/all_to_all | solution.py:48
